TPU v7x, 512 devices: a whole 4x4x16 slice. The times are simulated.
512 devices in a mesh: row: 16 (over x, y), col: 32 (over z, core).
Axes of the slice: x: 4, y: 4, z: 16, core: 2. Of those that a mesh axis runs over, the one named last changes fastest.
Arguments:
- field: bfloat16 [384, 256, 1024], P('row', 'col'), may hold values from -6 to 6
- mix: bfloat16 [1024, 1024], replicated, may hold values from -0.1875 to 0.1875
- stencil: float32 [2, 3, 3], replicated, may hold values from -2.5 to 2.5
- spectral: float32 [2, 8, 8, 1024], replicated, may hold values from -2.5 to 2.5
- cotangent: bfloat16 [384, 256, 1024], P('row', 'col'), may hold values from -6 to 6
Outputs:
- layer_out: bfloat16 [384, 256, 1024], P('row', 'col')
- grad_field: bfloat16 [384, 256, 1024], P('row', 'col')
All inputs are finite; a program needn't handle non-finite values.
Results may differ from a plain program's by a relative error of at most 0.0055.
The roundings to bfloat16 on the way count: a program that leaves them out, or rounds other values in their place, can miss the bound.
Values may be sent and summed in bfloat16 or wider, within the bound.
No kernel may reach another device: no remote copies, remote signals or barrier semaphores. Data moves between devices by JAX's collectives and lax.ppermute only.
A program may use at most 64 MiB of HBM per device.

v0:
```python
import math

import jax
import jax.numpy as jnp
import numpy as np
from jax import lax
from jax.sharding import PartitionSpec as P

CH = 64
K = 4
LEVELS = 2
MODES = 8


def with_halo(block, sides, width):
    for axis, dim in sides:
        count = lax.axis_size(axis)
        forward = [(i, i + 1) for i in range(count - 1)]
        forward.append((count - 1, 0))
        backward = [(target, source) for source, target in forward]
        low = lax.ppermute(
            lax.slice_in_dim(block, block.shape[dim] - width, None, axis=dim), axis, forward
        )
        high = lax.ppermute(lax.slice_in_dim(block, 0, width, axis=dim), axis, backward)
        block = jnp.concatenate([low, block, high], axis=dim)
    return block


def shifted_legendre(order_count):
    length = order_count + 1
    polys = [np.zeros(length), np.zeros(length)]
    polys[0][0] = 1.0
    polys[1][0] = -1.0
    polys[1][1] = 2.0
    for degree in range(1, order_count):
        times_t = np.zeros(length)
        times_t[1:] = 2.0 * polys[degree][:-1]
        times_t = times_t - polys[degree]
        polys.append(((2.0 * degree + 1.0) * times_t - degree * polys[degree - 1]) / (degree + 1.0))
    return [np.sqrt(2.0 * degree + 1.0) * polys[degree] for degree in range(order_count)]


def integrate_product(first, second):
    total = 0.0
    for power_a in range(first.shape[0]):
        for power_b in range(second.shape[0]):
            total = total + first[power_a] * second[power_b] / (power_a + power_b + 1.0)
    return total


def two_scale(order_count):
    polys = shifted_legendre(order_count)
    length = polys[0].shape[0]
    left_half = np.zeros((order_count, order_count))
    right_half = np.zeros((order_count, order_count))
    for out_index in range(order_count):
        coeffs = polys[out_index]
        halved = np.array([coeffs[power] * 0.5**power for power in range(length)])
        moved = np.zeros(length)
        for power in range(length):
            for lower in range(power + 1):
                moved[lower] = moved[lower] + coeffs[power] * 0.5**power * math.comb(power, lower)
        for in_index in range(order_count):
            left_half[out_index, in_index] = integrate_product(halved, polys[in_index]) / np.sqrt(
                2.0
            )
            right_half[out_index, in_index] = integrate_product(moved, polys[in_index]) / np.sqrt(
                2.0
            )
    scaling_rows = np.concatenate([left_half, right_half], axis=1)
    vectors = [scaling_rows[out_index] for out_index in range(order_count)]
    wavelet_rows = []
    for out_index in range(order_count):
        vector = np.zeros(2 * order_count)
        vector[out_index] = 1.0
        vector[order_count + out_index] = -1.0
        for earlier in vectors:
            vector = vector - np.dot(earlier, vector) * earlier
        vector = vector / np.sqrt(np.dot(vector, vector))
        vectors.append(vector)
        wavelet_rows.append(vector)
    filter_bank = np.stack([scaling_rows, np.stack(wavelet_rows)]).reshape(
        2, order_count, 2, order_count
    )
    return jnp.asarray(filter_bank, jnp.float32)


def decompose(state, filter_bank):
    height, breadth = (state.shape[0], state.shape[1])
    blocks = state.reshape(height // 2, 2, breadth // 2, 2, K, K, CH)
    parts = jnp.einsum(
        "xmak,ynbl,iajbklc->ijxymnc",
        filter_bank,
        filter_bank,
        blocks,
        precision=lax.Precision.HIGHEST,
    )
    parts = parts.reshape(height // 2, breadth // 2, 4, K * K * CH)
    return (parts[:, :, 0], parts[:, :, 1:])


def reconstruct(coarse, details, filter_bank):
    height, breadth = (coarse.shape[0], coarse.shape[1])
    parts = jnp.concatenate([coarse[:, :, None], details], axis=2).reshape(
        height, breadth, 2, 2, K, K, CH
    )
    blocks = jnp.einsum(
        "xmak,ynbl,ijxymnc->iajbklc",
        filter_bank,
        filter_bank,
        parts,
        precision=lax.Precision.HIGHEST,
    )
    return blocks.reshape(2 * height, 2 * breadth, K * K * CH)


def apply_taps(padded, taps, direction):
    height = padded.shape[0] - 2
    breadth = padded.shape[1] - 2
    total = jnp.zeros((height, breadth) + padded.shape[2:], jnp.float32)
    for shift_row in (-1, 0, 1):
        for shift_col in (-1, 0, 1):
            start_row = 1 + direction * shift_row
            start_col = 1 + direction * shift_col
            moved = padded[start_row : start_row + height, start_col : start_col + breadth]
            total = total + taps[shift_row + 1, shift_col + 1] * moved
    return total


def mode_basis(row_start, col_start, rows_here, cols_here, rows_all, cols_all):
    row_pos = row_start + lax.iota(jnp.int32, rows_here)
    col_pos = col_start + lax.iota(jnp.int32, cols_here)
    freqs = lax.iota(jnp.int32, MODES)
    numer = (
        freqs[:, None, None, None] * row_pos[None, None, :, None] * cols_all
        + freqs[None, :, None, None] * col_pos[None, None, None, :] * rows_all
    ) % (rows_all * cols_all)
    angles = numer.astype(jnp.float32) * (2.0 * math.pi / (rows_all * cols_all))
    return jnp.stack([jnp.cos(angles), jnp.sin(angles)]).reshape(
        2 * MODES * MODES, rows_here * cols_here
    )


def mix_detail(pre_act, mix):
    hidden = jax.nn.gelu(pre_act).astype(jnp.bfloat16)
    width = hidden.shape[-1]
    return jnp.dot(hidden.reshape(-1, width), mix, preferred_element_type=jnp.float32).reshape(
        pre_act.shape
    )


def project(basis, state):
    width = state.shape[-1]
    return jnp.dot(basis, state.reshape(-1, width), precision=lax.Precision.HIGHEST)


def expand(basis, coeffs, rows_here, cols_here):
    width = coeffs.shape[-1]
    return jnp.dot(basis.T, coeffs, precision=lax.Precision.HIGHEST).reshape(
        rows_here, cols_here, width
    )


def descend(cotangent, filter_bank):
    grad_state = cotangent.astype(jnp.float32)
    fines = []
    for level_index in range(LEVELS):
        grad_state, fine = decompose(grad_state, filter_bank)
        fines.append(fine.astype(jnp.bfloat16))
    return (grad_state, fines)


def body(field, mix, stencil, spectral, cotangent):
    filter_bank = two_scale(K)
    width = field.shape[2]
    activations = []
    state = field.astype(jnp.float32)
    for level_index in range(LEVELS):
        state, detail = decompose(state, filter_bank)
        padded_detail = with_halo(detail.astype(jnp.bfloat16), (("row", 0), ("col", 1)), 1)
        activations.append(apply_taps(padded_detail, stencil[level_index], 1))
    coarse_rows, coarse_cols = (state.shape[0], state.shape[1])
    rows_all = coarse_rows * lax.axis_size("row")
    cols_all = coarse_cols * lax.axis_size("col")
    basis = mode_basis(
        lax.axis_index("row") * coarse_rows,
        lax.axis_index("col") * coarse_cols,
        coarse_rows,
        coarse_cols,
        rows_all,
        cols_all,
    )
    scale = 1.0 / math.sqrt(rows_all * cols_all)
    gains = spectral.reshape(-1, width)
    modes = lax.psum(project(basis, state) * scale, ("row", "col"))
    upward = expand(basis, gains * modes, coarse_rows, coarse_cols)
    for level_index in reversed(range(LEVELS)):
        upward = reconstruct(upward, mix_detail(activations[level_index], mix), filter_bank)
    layer_out = upward.astype(jnp.bfloat16)
    grad_state, fines = descend(cotangent, filter_bank)
    back_modes = lax.psum(project(basis, grad_state), ("row", "col"))
    downward = expand(basis, gains * back_modes, coarse_rows, coarse_cols) * scale
    for level_index in reversed(range(LEVELS)):
        pre_act = activations[level_index]
        _, pullback = jax.vjp(jax.nn.gelu, pre_act)
        pre_grad = jnp.dot(
            fines[level_index].reshape(-1, width), mix.T, preferred_element_type=jnp.float32
        ).reshape(pre_act.shape)
        act_grad = pullback(pre_grad)[0].astype(jnp.bfloat16)
        padded_grad = with_halo(act_grad, (("row", 0), ("col", 1)), 1)
        downward = reconstruct(
            downward, apply_taps(padded_grad, stencil[level_index], -1), filter_bank
        )
    return (layer_out, downward.astype(jnp.bfloat16))


def solution(mesh):
    placed = (P("row", "col", None), P(), P(), P(), P("row", "col", None))
    return jax.shard_map(
        body,
        mesh=mesh,
        in_specs=placed,
        out_specs=(P("row", "col", None), P("row", "col", None)),
        check_vma=False,
    )
```

profile of v0, /device:TPU:1, one launch (start us, length us, event | category | flops | bytes accessed | tf_op | source)
XLA Modules:
  0.0 570.7 jit_solution(8216097757973426354)
XLA Ops:
  7.2 2.4 reshape.162
  9.6 2.5 convolution_bitcast_fusion.1
  12.1 2.9 fusion.20
  16.6 2.6 reshape.163
  22.9 4.0 collective-permute-start
  26.9 5.6 collective-permute-start.1
  35.7 6.9 %collective-permute-start.5 = (bf16[1,4,3,1024]{3,0,2,1:T(2,128)(2,1)}, bf16[1,4,3,1024]{3,0,2,1:T(2,128)(2,1)}, u32[]{:S(2)}, u32[]{:S(2)}) collective-permute-start(bf16[1,4,3,1024]{3,0,2,1:T(2,128)(2,1)} %get-tuple-element.7), channel_id=1, source_target_pairs={{32,0},{64,32},{96,64},{128,96},{160,128},{192,160},{224,192},{256... | collective-permute-start | bytes 73736 | tf_op jit(solution)/shard_map/ppermute | solution.py:24
  47.4 2.9 fusion.26
  51.8 2.8 reshape.168
  67.3 3.2 collective-permute-start.2
  70.5 3.9 collective-permute-start.3
  75.2 2.9 collective-permute-start.7
  79.1 6.4 %multiply_add_fusion.3 = f32[6,2,3,1024]{3,0,2,1:T(8,128)S(1)} fusion(bf16[6,2,3,1024]{3,0,2,1:T(8,128)(2,1)S(1)} %slice.367, bf16[8,3,3,1024]{3,0,2,1:T(8,128)(2,1)S(1)} %get-tuple-element.21, bf16[1,2,3,1024]{3,0,2,1:T(2,128)(2,1)} %collective-permute-done.1, bf16[8,3,3,1024]{3,0,2,1:T(8,128)(2,1)S(1)} %get-tuple-element.20, ...), kind=kLoop, calls=%fused_computation.104 | loop fusion | flops 1179648 | bytes 688164 | tf_op jit(solution)/shard_map/add | solution.py:126
  88.3 6.7 %collective-permute-start.9 = (bf16[1,2,3,1024]{3,0,2,1:T(2,128)(2,1)S(1)}, bf16[1,2,3,1024]{3,0,2,1:T(2,128)(2,1)S(1)}, u32[]{:S(2)}, u32[]{:S(2)}) collective-permute-start(bf16[1,2,3,1024]{3,0,2,1:T(2,128)(2,1)S(1)} %get-tuple-element.27), channel_id=1, source_target_pairs={{32,0},{64,32},{96,64},{128,96},{160,128},{192,160},{224,192},{256... | collective-permute-start | bytes 36872 | tf_op jit(solution)/shard_map/ppermute | solution.py:24
  96.3 3.8 collective-permute-start.10
  101.4 7.4 %multiply_add_fusion.1 = f32[12,4,3,1024]{3,0,2,1:T(8,128)S(1)} fusion(bf16[12,4,3,1024]{3,0,2,1:T(8,128)(2,1)S(1)} %slice.378, bf16[14,5,3,1024]{3,0,2,1:T(8,128)(2,1)S(1)} %get-tuple-element.13, bf16[1,4,3,1024]{3,0,2,1:T(2,128)(2,1)} %collective-permute-done.5, bf16[14,5,3,1024]{3,0,2,1:T(8,128)(2,1)S(1)} %get-tuple-element.12, ...), kind=kLoop, calls=%fused_computation.61 | loop fusion | flops 4718592 | bytes 2703396 | tf_op jit(solution)/shard_map/add | solution.py:126
  113.6 7.7 %collective-permute-start.13 = (bf16[1,4,3,1024]{3,0,2,1:T(2,128)(2,1)S(1)}, bf16[1,4,3,1024]{3,0,2,1:T(2,128)(2,1)S(1)}, u32[]{:S(2)}, u32[]{:S(2)}) collective-permute-start(bf16[1,4,3,1024]{3,0,2,1:T(2,128)(2,1)S(1)} %get-tuple-element.17), channel_id=1, source_target_pairs={{32,0},{64,32},{96,64},{128,96},{160,128},{192,160},{224,192},{256... | collective-permute-start | bytes 73736 | tf_op jit(solution)/shard_map/ppermute | solution.py:24
  123.9 5.6 multiply_add_fusion.2
  130.0 7.5 %multiply_add_fusion = f32[12,4,3,1024]{3,0,2,1:T(8,128)} fusion(bf16[12,4,3,1024]{3,0,2,1:T(8,128)(2,1)S(1)} %fusion.49, bf16[14,5,3,1024]{3,0,2,1:T(8,128)(2,1)S(1)} %get-tuple-element.9, bf16[1,4,3,1024]{3,0,2,1:T(2,128)(2,1)S(1)} %collective-permute-done.12, bf16[14,5,3,1024]{3,0,2,1:T(8,128)(2,1)S(1)} %get-tuple-element.8, ...), kind=kLoop, calls=%fused_computation.59 | loop fusion | flops 4718592 | bytes 2703396 | tf_op jit(solution)/shard_map/add | solution.py:126
  137.5 392.5 %all-reduce.3.cloned.1.call-done = (f32[128,1024]{1,0:T(8,128)}, f32[128,1024]{1,0:T(8,128)}) async-done(((f32[128,1024]{1,0:T(8,128)}, f32[128,1024]{1,0:T(8,128)}), (f32[128,1024]{1,0:T(8,128)}, f32[128,1024]{1,0:T(8,128)})) %all-reduce.3.cloned.1.call-update) | async-done | bytes 1048592 | tf_op jit(solution)/shard_map/psum | solution.py:195
  538.4 4.3 fusion.29
  542.7 3.0 fusion.39
  554.7 4.3 fusion.23
  559.0 3.0 fusion.36
  (134 shorter events, 61.2 us)
Async XLA Ops:
  7.2 78.3 %copy-start = (bf16[1024,1024]{1,0:T(8,128)(2,1)S(1)}, bf16[1024,1024]{1,0:T(8,128)(2,1)}, u32[]{:S(2)}) copy-start(bf16[1024,1024]{1,0:T(8,128)(2,1)} %param.7) | copy-start | bytes 6291460
  7.2 522.8 %all-reduce.3.cloned.1.call-start = ((), (), s32[]{:S(2)}) async-start(), calls=%async_computation | async-start | bytes 2097152 | tf_op jit(solution)/shard_map/psum | solution.py:195
  22.1 23.4 %copy-start.12 = (f32[2,4,2,4,1,1,1,1]{3,1,2,7,6,5,4,0:T(4,128)S(1)}, f32[2,4,2,4,1,1,1,1]{3,1,2,7,6,5,4,0:T(4,128)}, u32[]{:S(2)}) copy-start(f32[2,4,2,4,1,1,1,1]{3,1,2,7,6,5,4,0:T(4,128)} %constant.57) | copy-start | bytes 772
  22.2 25.2 %copy-start.4 = (bf16[6,2,4,1024]{3,0,2,1:T(8,128)(2,1)}, bf16[6,2,4,1024]{3,0,2,1:T(8,128)(2,1)S(1)}, u32[]{:S(2)}) copy-start(bf16[6,2,4,1024]{3,0,2,1:T(8,128)(2,1)S(1)} %copy.252) | copy-start | bytes 294916
  22.9 43.5 %collective-permute-start = (bf16[1,2,3,1024]{3,0,2,1:T(2,128)(2,1)}, bf16[1,2,3,1024]{3,0,2,1:T(2,128)(2,1)S(1)}, u32[]{:S(2)}, u32[]{:S(2)}) collective-permute-start(bf16[1,2,3,1024]{3,0,2,1:T(2,128)(2,1)} %get-tuple-element.22), channel_id=1, source_target_pairs={{0,32},{32,64},{64,96},{96,128},{128,160},{160,192},{192,224},{224... | collective-permute-start | bytes 36872 | tf_op jit(solution)/shard_map/ppermute | solution.py:21
  26.9 39.5 %collective-permute-start.1 = (bf16[1,2,3,1024]{3,0,2,1:T(2,128)(2,1)}, bf16[1,2,3,1024]{3,0,2,1:T(2,128)(2,1)}, u32[]{:S(2)}, u32[]{:S(2)}) collective-permute-start(bf16[1,2,3,1024]{3,0,2,1:T(2,128)(2,1)} %get-tuple-element.23), channel_id=1, source_target_pairs={{32,0},{64,32},{96,64},{128,96},{160,128},{192,160},{224,192},{256... | collective-permute-start | bytes 36872 | tf_op jit(solution)/shard_map/ppermute | solution.py:24
  32.9 9.6 %copy-start.2 = (bf16[12,4,4,1024]{3,0,2,1:T(8,128)(2,1)}, bf16[12,4,4,1024]{3,0,2,1:T(8,128)(2,1)S(1)}, u32[]{:S(2)}) copy-start(bf16[12,4,4,1024]{3,0,2,1:T(8,128)(2,1)S(1)} %copy.251) | copy-start | bytes 1179652
  33.8 40.6 %collective-permute-start.4 = (bf16[1,4,3,1024]{3,0,2,1:T(2,128)(2,1)}, bf16[1,4,3,1024]{3,0,2,1:T(2,128)(2,1)S(1)}, u32[]{:S(2)}, u32[]{:S(2)}) collective-permute-start(bf16[1,4,3,1024]{3,0,2,1:T(2,128)(2,1)} %get-tuple-element.6), channel_id=1, source_target_pairs={{0,32},{32,64},{64,96},{96,128},{128,160},{160,192},{192,224},{224... | collective-permute-start | bytes 73736 | tf_op jit(solution)/shard_map/ppermute | solution.py:21
  35.7 38.7 %collective-permute-start.5 = (bf16[1,4,3,1024]{3,0,2,1:T(2,128)(2,1)}, bf16[1,4,3,1024]{3,0,2,1:T(2,128)(2,1)}, u32[]{:S(2)}, u32[]{:S(2)}) collective-permute-start(bf16[1,4,3,1024]{3,0,2,1:T(2,128)(2,1)} %get-tuple-element.7), channel_id=1, source_target_pairs={{32,0},{64,32},{96,64},{128,96},{160,128},{192,160},{224,192},{256... | collective-permute-start | bytes 73736 | tf_op jit(solution)/shard_map/ppermute | solution.py:24
  57.6 5.9 %copy-start.5 = (bf16[6,2,4,1024]{3,0,2,1:T(8,128)(2,1)S(1)}, bf16[6,2,4,1024]{3,0,2,1:T(8,128)(2,1)}, u32[]{:S(2)}) copy-start(bf16[6,2,4,1024]{3,0,2,1:T(8,128)(2,1)} %copy-done.4) | copy-start | bytes 294916
  66.4 465.7 %copy-start.10 = (f32[6,2,128]{2,1,0:T(2,128)}, f32[6,2,128]{2,1,0:T(2,128)S(1)}, u32[]{:S(2)}) copy-start(f32[6,2,128]{2,1,0:T(2,128)S(1)} %dot_general.79) | copy-start | bytes 18436
  67.3 10.9 %collective-permute-start.2 = (bf16[8,1,3,1024]{3,0,2,1:T(8,128)(2,1)S(1)}, bf16[8,1,3,1024]{3,0,2,1:T(8,128)(2,1)S(1)}, u32[]{:S(2)}, u32[]{:S(2)}) collective-permute-start(bf16[8,1,3,1024]{3,0,2,1:T(8,128)(2,1)S(1)} %get-tuple-element.28), channel_id=1, source_target_pairs={{0,1},{1,2},{2,3},{3,4},{4,5},{5,6},{6,7},{7,8},{8,9},{9,10},{10,1... | collective-permute-start | bytes 147464 | tf_op jit(solution)/shard_map/ppermute | solution.py:21
  70.5 7.7 %collective-permute-start.3 = (bf16[8,1,3,1024]{3,0,2,1:T(8,128)(2,1)S(1)}, bf16[8,1,3,1024]{3,0,2,1:T(8,128)(2,1)S(1)}, u32[]{:S(2)}, u32[]{:S(2)}) collective-permute-start(bf16[8,1,3,1024]{3,0,2,1:T(8,128)(2,1)S(1)} %get-tuple-element.29), channel_id=1, source_target_pairs={{1,0},{2,1},{3,2},{4,3},{5,4},{6,5},{7,6},{8,7},{9,8},{10,9},{11,1... | collective-permute-start | bytes 147464 | tf_op jit(solution)/shard_map/ppermute | solution.py:24
  75.2 24.9 %collective-permute-start.6 = (bf16[14,1,3,1024]{3,0,2,1:T(8,128)(2,1)S(1)}, bf16[14,1,3,1024]{3,0,2,1:T(8,128)(2,1)S(1)}, u32[]{:S(2)}, u32[]{:S(2)}) collective-permute-start(bf16[14,1,3,1024]{3,0,2,1:T(8,128)(2,1)S(1)} %get-tuple-element.14), channel_id=1, source_target_pairs={{0,1},{1,2},{2,3},{3,4},{4,5},{5,6},{6,7},{7,8},{8,9},{9,10},{10,1... | collective-permute-start | bytes 258056 | tf_op jit(solution)/shard_map/ppermute | solution.py:21
  75.2 24.9 %collective-permute-start.7 = (bf16[14,1,3,1024]{3,0,2,1:T(8,128)(2,1)S(1)}, bf16[14,1,3,1024]{3,0,2,1:T(8,128)(2,1)S(1)}, u32[]{:S(2)}, u32[]{:S(2)}) collective-permute-start(bf16[14,1,3,1024]{3,0,2,1:T(8,128)(2,1)S(1)} %get-tuple-element.15), channel_id=1, source_target_pairs={{1,0},{2,1},{3,2},{4,3},{5,4},{6,5},{7,6},{8,7},{9,8},{10,9},{11,1... | collective-permute-start | bytes 258056 | tf_op jit(solution)/shard_map/ppermute | solution.py:24
  86.4 9.8 %collective-permute-start.8 = (bf16[1,2,3,1024]{3,0,2,1:T(2,128)(2,1)S(1)}, bf16[1,2,3,1024]{3,0,2,1:T(2,128)(2,1)S(1)}, u32[]{:S(2)}, u32[]{:S(2)}) collective-permute-start(bf16[1,2,3,1024]{3,0,2,1:T(2,128)(2,1)S(1)} %get-tuple-element.26), channel_id=1, source_target_pairs={{0,32},{32,64},{64,96},{96,128},{128,160},{160,192},{192,224},{224... | collective-permute-start | bytes 36872 | tf_op jit(solution)/shard_map/ppermute | solution.py:21
  88.3 7.9 %collective-permute-start.9 = (bf16[1,2,3,1024]{3,0,2,1:T(2,128)(2,1)S(1)}, bf16[1,2,3,1024]{3,0,2,1:T(2,128)(2,1)S(1)}, u32[]{:S(2)}, u32[]{:S(2)}) collective-permute-start(bf16[1,2,3,1024]{3,0,2,1:T(2,128)(2,1)S(1)} %get-tuple-element.27), channel_id=1, source_target_pairs={{32,0},{64,32},{96,64},{128,96},{160,128},{192,160},{224,192},{256... | collective-permute-start | bytes 36872 | tf_op jit(solution)/shard_map/ppermute | solution.py:24
  96.3 25.0 %collective-permute-start.10 = (bf16[8,1,3,1024]{3,0,2,1:T(8,128)(2,1)S(1)}, bf16[8,1,3,1024]{3,0,2,1:T(8,128)(2,1)S(1)}, u32[]{:S(2)}, u32[]{:S(2)}) collective-permute-start(bf16[8,1,3,1024]{3,0,2,1:T(8,128)(2,1)S(1)} %get-tuple-element.24), channel_id=1, source_target_pairs={{1,0},{2,1},{3,2},{4,3},{5,4},{6,5},{7,6},{8,7},{9,8},{10,9},{11,1... | collective-permute-start | bytes 147464 | tf_op jit(solution)/shard_map/ppermute | solution.py:24
  100.1 21.2 %collective-permute-start.11 = (bf16[8,1,3,1024]{3,0,2,1:T(8,128)(2,1)S(1)}, bf16[8,1,3,1024]{3,0,2,1:T(8,128)(2,1)S(1)}, u32[]{:S(2)}, u32[]{:S(2)}) collective-permute-start(bf16[8,1,3,1024]{3,0,2,1:T(8,128)(2,1)S(1)} %get-tuple-element.25), channel_id=1, source_target_pairs={{0,1},{1,2},{2,3},{3,4},{4,5},{5,6},{6,7},{7,8},{8,9},{9,10},{10,1... | collective-permute-start | bytes 147464 | tf_op jit(solution)/shard_map/ppermute | solution.py:21
  111.7 9.8 %collective-permute-start.12 = (bf16[1,4,3,1024]{3,0,2,1:T(2,128)(2,1)S(1)}, bf16[1,4,3,1024]{3,0,2,1:T(2,128)(2,1)S(1)}, u32[]{:S(2)}, u32[]{:S(2)}) collective-permute-start(bf16[1,4,3,1024]{3,0,2,1:T(2,128)(2,1)S(1)} %get-tuple-element.16), channel_id=1, source_target_pairs={{0,32},{32,64},{64,96},{96,128},{128,160},{160,192},{192,224},{224... | collective-permute-start | bytes 73736 | tf_op jit(solution)/shard_map/ppermute | solution.py:21
  113.6 8.4 %collective-permute-start.13 = (bf16[1,4,3,1024]{3,0,2,1:T(2,128)(2,1)S(1)}, bf16[1,4,3,1024]{3,0,2,1:T(2,128)(2,1)S(1)}, u32[]{:S(2)}, u32[]{:S(2)}) collective-permute-start(bf16[1,4,3,1024]{3,0,2,1:T(2,128)(2,1)S(1)} %get-tuple-element.17), channel_id=1, source_target_pairs={{32,0},{64,32},{96,64},{128,96},{160,128},{192,160},{224,192},{256... | collective-permute-start | bytes 73736 | tf_op jit(solution)/shard_map/ppermute | solution.py:24
  122.1 7.4 %collective-permute-start.14 = (bf16[14,1,3,1024]{3,0,2,1:T(8,128)(2,1)S(1)}, bf16[14,1,3,1024]{3,0,2,1:T(8,128)(2,1)S(1)}, u32[]{:S(2)}, u32[]{:S(2)}) collective-permute-start(bf16[14,1,3,1024]{3,0,2,1:T(8,128)(2,1)S(1)} %get-tuple-element.10), channel_id=1, source_target_pairs={{1,0},{2,1},{3,2},{4,3},{5,4},{6,5},{7,6},{8,7},{9,8},{10,9},{11,1... | collective-permute-start | bytes 258056 | tf_op jit(solution)/shard_map/ppermute | solution.py:24
  123.5 6.1 %collective-permute-start.15 = (bf16[14,1,3,1024]{3,0,2,1:T(8,128)(2,1)S(1)}, bf16[14,1,3,1024]{3,0,2,1:T(8,128)(2,1)S(1)}, u32[]{:S(2)}, u32[]{:S(2)}) collective-permute-start(bf16[14,1,3,1024]{3,0,2,1:T(8,128)(2,1)S(1)} %get-tuple-element.11), channel_id=1, source_target_pairs={{0,1},{1,2},{2,3},{3,4},{4,5},{5,6},{6,7},{7,8},{8,9},{9,10},{10,1... | collective-permute-start | bytes 258056 | tf_op jit(solution)/shard_map/ppermute | solution.py:21
  130.0 400.1 %copy-start.7 = (f32[2,8,8,1024]{3,2,1,0:T(8,128)S(1)}, f32[2,8,8,1024]{3,2,1,0:T(8,128)}, u32[]{:S(2)}) copy-start(f32[2,8,8,1024]{3,2,1,0:T(8,128)} %param.9) | copy-start | bytes 1572868
  (7 other events, 22.8 us)
Sparse Core Ops, SparseCore 0:
  62.2 467.8 all-reduce.2
where the time goes:
time: 580 us; the launch traced here: 571 us
  waiting for transfers between devices  393 us (68%)
  starting transfers between devices  52.1 us (9%)
  matrix products  39.9 us (7%)
  other arithmetic  37.5 us (6%)
  local copies, waits for them, and re-layouts  33 us (6%)
  between operations  15 us (3%)
    psum x1, waiting for transfers between devices, body(): modes = lax.psum(project(basis, state) * scale, ('row', 'col'))  393 us
    ppermute x8, starting transfers between devices, with_halo(): lax.ppermute(lax.slice_in_dim(block, 0, width, axis=dim), axis, backward)  38.8 us
    add x4, other arithmetic, apply_taps(): total = total + taps[shift_row + 1, shift_col + 1] * moved  27 us
    dot_general x8, matrix products, reconstruct(): jnp.einsum('xmak,ynbl,ijxymnc->iajbklc', filter_bank, filter_bank, parts,...  17.9 us
    dot_general x8, matrix products, decompose(): jnp.einsum('xmak,ynbl,iajbklc->ijxymnc', filter_bank, filter_bank, blocks...  13.6 us
    ppermute x8, starting transfers between devices, with_halo(): lax.ppermute(lax.slice_in_dim(block, block.shape[dim] - width, None, axis...  13.4 us
  transfers between devices with their start and end apart: 17, of which 2 were waited for; matrix products, arithmetic and copies ran while one was open for 11% of the time, Pallas kernels for 0%

commit v1 on v0

v1 whole, which is shorter than its diff:
```python
import functools
import math

import jax
import jax.numpy as jnp
import ml_dtypes
import numpy as np
from jax import lax
from jax.experimental import pallas as pl
from jax.experimental.pallas import tpu as pltpu
from jax.sharding import PartitionSpec as P

CH = 64
K = 4
MODES = 8
F = 1024
BF = jnp.bfloat16
F32 = jnp.float32
QW = K * CH

FI, FJ = 24, 8
H1, W1 = 12, 4
H2, W2 = 6, 2
G1, G2 = 64, 16
SIDES = [(-1, 0), (1, 0), (0, -1), (0, 1)]


def shifted_legendre(order_count):
    length = order_count + 1
    polys = [np.zeros(length), np.zeros(length)]
    polys[0][0] = 1.0
    polys[1][0] = -1.0
    polys[1][1] = 2.0
    for degree in range(1, order_count):
        times_t = np.zeros(length)
        times_t[1:] = 2.0 * polys[degree][:-1]
        times_t = times_t - polys[degree]
        polys.append(((2.0 * degree + 1.0) * times_t - degree * polys[degree - 1]) / (degree + 1.0))
    return [np.sqrt(2.0 * degree + 1.0) * polys[degree] for degree in range(order_count)]


def integrate_product(first, second):
    total = 0.0
    for power_a in range(first.shape[0]):
        for power_b in range(second.shape[0]):
            total = total + first[power_a] * second[power_b] / (power_a + power_b + 1.0)
    return total


def two_scale(order_count):
    polys = shifted_legendre(order_count)
    length = polys[0].shape[0]
    left_half = np.zeros((order_count, order_count))
    right_half = np.zeros((order_count, order_count))
    for out_index in range(order_count):
        coeffs = polys[out_index]
        halved = np.array([coeffs[power] * 0.5**power for power in range(length)])
        moved = np.zeros(length)
        for power in range(length):
            for lower in range(power + 1):
                moved[lower] = moved[lower] + coeffs[power] * 0.5**power * math.comb(power, lower)
        for in_index in range(order_count):
            left_half[out_index, in_index] = integrate_product(halved, polys[in_index]) / np.sqrt(2.0)
            right_half[out_index, in_index] = integrate_product(moved, polys[in_index]) / np.sqrt(2.0)
    scaling_rows = np.concatenate([left_half, right_half], axis=1)
    vectors = [scaling_rows[out_index] for out_index in range(order_count)]
    wavelet_rows = []
    for out_index in range(order_count):
        vector = np.zeros(2 * order_count)
        vector[out_index] = 1.0
        vector[order_count + out_index] = -1.0
        for earlier in vectors:
            vector = vector - np.dot(earlier, vector) * earlier
        vector = vector / np.sqrt(np.dot(vector, vector))
        vectors.append(vector)
        wavelet_rows.append(vector)
    return np.stack([scaling_rows, np.stack(wavelet_rows)]).reshape(2, order_count, 2, order_count)


BANK = two_scale(K)
BANK[np.abs(BANK) < 1e-12] = 0.0


def halves(array):
    high = np.asarray(array, np.float32).astype(ml_dtypes.bfloat16)
    low = (np.asarray(array, np.float64) - high.astype(np.float64)).astype(ml_dtypes.bfloat16)
    return high, low


COL_FILTER = np.kron(BANK.transpose(2, 3, 0, 1).reshape(2 * K, 2 * K), np.eye(CH))


def rho(i, j):
    return ((i % 2) * 2 + j % 2) * G2 + (i // 2) * W2 + j // 2


def local_row(kind, i, j):
    if kind == "d1":
        return rho(i, j)
    if kind == "d2":
        return G1 + i * W2 + j
    if kind == "b1":
        return G1 + G2 + rho(i, j)
    return 2 * G1 + G2 + i * W2 + j


LOC = 2 * (G1 + G2)
REACH = {"d1": (H1, W1, 2), "d2": (H2, W2, 2), "b1": (H1, W1, 1), "b2": (H2, W2, 1)}


TWICE = np.einsum("pbm,mak->pbak", BANK[0], BANK[0]).reshape(K, 4, K)
COARSE_LEFT = np.zeros((K, 4, K, G2, FI * FJ))
for i_ in range(FI):
    for j_ in range(FJ):
        COARSE_LEFT[:, j_ % 4, :, (i_ // 4) * W2 + j_ // 4, i_ * FJ + j_] = TWICE[:, i_ % 4, :].T
COARSE_LEFT = COARSE_LEFT.reshape(K, 4 * K * G2, FI * FJ)
COARSE_RIGHT = np.kron(TWICE.transpose(1, 2, 0).reshape(4 * K, K), np.eye(CH))


def gather_table():
    table = np.zeros((4 * G1, FI * FJ), np.float32)
    for i in range(FI):
        for j in range(FJ):
            table[((i % 2) * 2 + j % 2) * G1 + rho(i // 2, j // 2), i * FJ + j] = 1.0
    return table


COLUMN = {}
for kind_, (height_, breadth_, _) in REACH.items():
    for i_ in range(height_):
        for j_ in range(breadth_):
            COLUMN[(kind_, i_, j_)] = local_row(kind_, i_, j_)


def message_plan():
    at, plan, starts = LOC, [], []
    for first in (0, 2):
        for dr, dc in SIDES[first : first + 2]:
            message = []
            for part in ("d", "b"):
                cells = []
                for kind, (height, breadth, reach) in REACH.items():
                    if kind[0] != part:
                        continue
                    rows, columns = range(-reach, height + reach), range(-reach, breadth + reach)
                    if dr:
                        rows = rows[:reach] if dr < 0 else rows[-reach:]
                        columns = columns[reach:-reach]
                    else:
                        columns = columns[:reach] if dc < 0 else columns[-reach:]
                    for i in rows:
                        for j in columns:
                            source = COLUMN[(kind, i - dr * height, j - dc * breadth)]
                            cells.append((kind, i, j, source))
                message.append(cells + [None] * (-len(cells) % 8))
            plan.append(message)
            starts.append(at)
            at += len(message[0]) + len(message[1])
        for start, message in zip(starts[first:], plan[first:]):
            for n, cell in enumerate(message[0] + message[1]):
                if cell:
                    COLUMN[cell[:3]] = start + n
    return plan, starts, at


PLAN, MSG_AT, KNOWN = message_plan()
MSG_ROWS = [end - start for start, end in zip(MSG_AT, MSG_AT[1:] + [KNOWN])]
MSG_CUT = [len(message[0]) for message in PLAN]
SIDE_END = MSG_AT[2]
SEND_SIDE = np.zeros((SIDE_END - LOC, LOC), np.float32)
SEND_ENDS = np.zeros((KNOWN - SIDE_END, SIDE_END), np.float32)
for n_, message_ in enumerate(PLAN):
    for m_, cell_ in enumerate(message_[0] + message_[1]):
        if cell_ and n_ < 2:
            SEND_SIDE[MSG_AT[n_] - LOC + m_, cell_[3]] = 1.0
        elif cell_:
            SEND_ENDS[MSG_AT[n_] - SIDE_END + m_, cell_[3]] = 1.0

STACKED = {}
STACK_ROWS = []
for part_ in (0, 1):
    at_ = G1 + G2
    for kind_, (height_, breadth_, _) in REACH.items():
        if kind_[0] == "db"[part_]:
            for i_ in range(height_):
                for j_ in range(breadth_):
                    STACKED[(kind_, i_, j_)] = local_row(kind_, i_, j_) - part_ * (G1 + G2)
    for message_ in PLAN:
        for m_, cell_ in enumerate(message_[part_]):
            if cell_:
                STACKED[cell_[:3]] = at_ + m_
        at_ += len(message_[part_])
    STACK_ROWS.append(at_)

INNER = G1 + G2
QROW = {}
for i_ in range(H1):
    for j_ in range(W1):
        QROW[(1, i_, j_)] = rho(i_, j_)
for i_ in range(H2):
    for j_ in range(W2):
        QROW[(2, i_, j_)] = G1 + i_ * W2 + j_
next_ = INNER
for level_, (height_, breadth_) in ((1, (H1, W1)), (2, (H2, W2))):
    for i_ in range(-1, height_ + 1):
        for j_ in range(-1, breadth_ + 1):
            if (level_, i_, j_) not in QROW:
                QROW[(level_, i_, j_)] = next_
                next_ += 1
QROWS = -(-next_ // 16) * 16

TAP_AT = np.full((QROWS, STACK_ROWS[0]), -1, np.int32)
PICK_BACK = np.zeros((QROWS, STACK_ROWS[1]), np.float32)
TAP_BACK = np.full((INNER, QROWS), -1, np.int32)
for (level_, i_, j_), q_ in QROW.items():
    PICK_BACK[q_, STACKED[("b%d" % level_, i_, j_)]] = 1.0
    for a_ in (-1, 0, 1):
        for b_ in (-1, 0, 1):
            tap_ = (level_ - 1) * 9 + (a_ + 1) * 3 + b_ + 1
            TAP_AT[q_, STACKED[("d%d" % level_, i_ + a_, j_ + b_)]] = tap_
            if q_ < INNER:
                TAP_BACK[q_, QROW[(level_, i_ - a_, j_ - b_)]] = tap_


def split(value):
    high = value.astype(BF)
    return high, (value - high.astype(F32)).astype(BF)


def mm(left, right):
    return jnp.dot(left, right, preferred_element_type=F32)


def rows_forward(parts, bands=(0, 1)):
    plus = [parts[0][k] + parts[1][k] for k in range(K)]
    minus = [parts[0][k] - parts[1][k] for k in range(K)]
    out = []
    for band in bands:
        outs = []
        for m in range(K):
            total = None
            for k in range(K):
                first, second = BANK[band, m, 0, k], BANK[band, m, 1, k]
                if first == 0.0:
                    continue
                term = (plus if first * second > 0 else minus)[k] * float(first)
                total = term if total is None else total + term
            outs.append(total)
        out.append(outs)
    return out


def rows_inverse(parts, bands=(0, 1)):
    out = [[None] * K, [None] * K]
    for k in range(K):
        same, other = None, None
        for band in bands:
            for m in range(K):
                first, second = BANK[band, m, 0, k], BANK[band, m, 1, k]
                if first == 0.0:
                    continue
                term = parts[band][m] * float(first)
                if first * second > 0:
                    same = term if same is None else same + term
                else:
                    other = term if other is None else other + term
        out[0][k] = same + other if other is not None else same
        out[1][k] = same - other if other is not None else same
    return out


def coarse_kernel(left_ref, wh_ref, wl_ref, field_ref, cot_ref, part_ref):
    count = K * G2
    found = []
    for source in (field_ref, cot_ref):
        total = None
        for k in range(K):
            term = mm(left_ref[k], source[:, k * QW : (k + 1) * QW])
            total = term if total is None else total + term
        found.append(total[: 4 * count] + total[4 * count :])
    state = None
    for j in range(4):
        piece = jnp.concatenate([part[j * count : (j + 1) * count] for part in found], axis=0)
        rows = slice(j * QW, (j + 1) * QW)
        term = times_filter(piece, wh_ref[rows], wl_ref[rows])
        state = term if state is None else state + term
    low_half = lax.broadcasted_iota(jnp.int32, (G2, 2 * CH), 1) < CH
    for m in range(K):
        for half in range(2):
            lanes = slice(half * 2 * CH, (half + 1) * 2 * CH)
            first = state[m * G2 : (m + 1) * G2, lanes]
            second = state[count + m * G2 : count + (m + 1) * G2, lanes]
            part_ref[m * K + 2 * half] = jnp.where(low_half, first, pltpu.roll(second, CH, 1))
            part_ref[m * K + 2 * half + 1] = jnp.where(low_half, pltpu.roll(first, CH, 1), second)


def analyze_kernel(stencil_ref, place_ref, field_ref, cot_ref, gather_ref, wh_ref, wl_ref, send_ref, tap_ref, tap_back_ref, places_ref, gains_ref, loc_ref, up_ref, down_ref, lead_ref, lead_back_ref, my_places_ref, my_gains_ref):
    gather = gather_ref[...]
    lefts = [[], []]
    for source in (field_ref, cot_ref):
        moved = mm(gather, source[...]).astype(BF)
        for a in range(2):
            for k in range(K):
                for b in range(2):
                    at = (a * 2 + b) * G1
                    lefts[b].append(moved[at : at + G1, k * QW : (k + 1) * QW])
    left = [jnp.concatenate(part, axis=0) for part in lefts]
    high = mm(left[0], wh_ref[: 2 * CH * 2]) + mm(left[1], wh_ref[2 * CH * 2 :])
    low = mm(left[0], wl_ref[: 2 * CH * 2]) + mm(left[1], wl_ref[2 * CH * 2 :])
    mixed = high + low
    lefts = [[], []]
    locs = []
    for n in range(2):
        parts = [[mixed[((n * 2 + a) * K + k) * G1 :][:G1] for k in range(K)] for a in range(2)]
        out = rows_forward(parts)
        detail = [out[0][m][:, QW:] for m in range(K)] + [out[1][m][:, :QW] for m in range(K)]
        detail += [out[1][m][:, QW:] for m in range(K)]
        locs.append(jnp.concatenate(detail, axis=1).astype(BF))
        for a in range(2):
            for k in range(K):
                for b in range(2):
                    at = (a * 2 + b) * G2
                    lefts[b].append(out[0][k][at : at + G2, :QW])
    mixed = None
    for b in range(2):
        high, low = split(jnp.concatenate(lefts[b], axis=0))
        rows = slice(b * QW, (b + 1) * QW)
        term = mm(high, wh_ref[rows]) + mm(low, wh_ref[rows]) + mm(high, wl_ref[rows])
        mixed = term if mixed is None else mixed + term
    for n in range(2):
        parts = [[mixed[((n * 2 + a) * K + k) * G2 :][:G2] for k in range(K)] for a in range(2)]
        out = rows_forward(parts)
        detail = [out[0][m][:, QW:] for m in range(K)] + [out[1][m][:, :QW] for m in range(K)]
        detail += [out[1][m][:, QW:] for m in range(K)]
        at = n * INNER
        loc_ref[at : at + G1, :] = locs[n]
        loc_ref[at + G1 : at + INNER, :] = jnp.concatenate(detail, axis=1).astype(BF)
    moved = mm(send_ref[...], loc_ref[...])
    up_ref[...] = moved[: MSG_ROWS[0]].astype(BF)
    down_ref[...] = moved[MSG_ROWS[0] :].astype(BF)
    up_ref.send()
    down_ref.send()
    loc_ref.send()
    taps = [stencil_ref[n] for n in range(18)]
    lead_ref[:QROWS], lead_ref[QROWS:] = split(tap_matrix(tap_ref[...], taps))
    lead_back_ref[:INNER], lead_back_ref[INNER:] = split(tap_matrix(tap_back_ref[...], taps))
    my_places_ref[...] = places_ref[...]
    gains = gains_ref[...]
    low_half = lax.broadcasted_iota(jnp.int32, gains.shape, 1) < CH
    even = (place_ref[0] % 2) == 0
    my_gains_ref[...] = jnp.where(low_half == even, gains, pltpu.roll(gains, CH, 1))


def stack(parts):
    return jnp.concatenate([part.astype(F32) for part in parts], axis=0).astype(BF)


def along_kernel(rows_ref, parts_ref, out_ref):
    out = mm3(rows_ref, parts_ref[...].reshape(-1, 2 * CH)).astype(BF)
    for n in range(out_ref.shape[0]):
        out_ref[n] = out


def ends_kernel(send_ref, loc_ref, up_ref, down_ref, left_ref, right_ref):
    known = jnp.concatenate([loc_ref[...], stack([up_ref[...], down_ref[...]])], axis=0)
    moved = mm(send_ref[...], known).astype(BF)
    left_ref[...] = moved[: MSG_ROWS[2]]
    right_ref[...] = moved[MSG_ROWS[2] :]


def modes_kernel(scale, across_ref, table_ref, rows_ref, gains_ref, parts_ref, out_ref):
    parts = parts_ref[...].reshape(-1, 2 * CH)
    modes = mm(across_ref[0], parts) + mm(across_ref[1], parts)
    wide = mm3(table_ref, gains_ref[...] * modes * scale)
    out_ref[...] = mm3(rows_ref, wide).reshape(out_ref.shape)


def mm3(left_ref, right):
    high, low = split(right)
    left_high = left_ref[0]
    return mm(left_high, high) + mm(left_ref[1], high) + mm(left_high, low)


def tap_matrix(at, taps):
    total = jnp.zeros(at.shape, F32)
    for n, tap in enumerate(taps):
        total = jnp.where(at == n, tap, total)
    return total


def detail_kernel(lead_ref, pick_ref, loc_ref, up_ref, down_ref, left_ref, right_ref, mix_ref, lead_back_ref, wh_ref, wl_ref, scatter_ref, out_ref, scratch):
    messages = [ref[...].astype(F32) for ref in (up_ref, down_ref, left_ref, right_ref)]
    details = [message[:cut] for message, cut in zip(messages, MSG_CUT)]
    others = [message[cut:] for message, cut in zip(messages, MSG_CUT)]
    details = jnp.concatenate([loc_ref[:INNER], stack(details)], axis=0)
    others = jnp.concatenate([loc_ref[INNER:], stack(others)], axis=0)
    lead, pick, lead_back = lead_ref[...], pick_ref[...], lead_back_ref[...]
    slope = math.sqrt(2.0 / math.pi)
    acts, derivatives, backs = [], [], []
    for band in range(3):
        lanes = slice(band * F, (band + 1) * F)
        found = mm(lead, details[:, lanes])
        pre = found[:QROWS] + found[QROWS:]
        square = pre * pre
        curve = jnp.tanh(slope * (pre + 0.044715 * (pre * square)))
        cdf = 0.5 * (1.0 + curve)
        acts.append((pre * cdf)[:INNER].astype(BF))
        derivatives.append(
            cdf + (0.5 * slope) * pre * (1.0 - curve * curve) * (1.0 + (3 * 0.044715) * square)
        )
        backs.append(mm(pick, others[:, lanes]).astype(BF))
    mix = mix_ref[...]
    mixed = mm(jnp.concatenate(acts, axis=0), mix)
    back = lax.dot_general(
        jnp.concatenate(backs, axis=0), mix, (((1,), (1,)), ((), ())), preferred_element_type=F32
    )
    for band in range(3):
        scratch[0, band] = mixed[band * INNER : (band + 1) * INNER]
        grad = (back[band * QROWS : (band + 1) * QROWS] * derivatives[band]).astype(BF)
        found = mm(lead_back, grad)
        scratch[1, band] = found[:INNER] + found[INNER:]
    found = synthesize(None, scratch, slice(G1, INNER), wh_ref, wl_ref)
    found = synthesize([place(out) for out in found], scratch, slice(0, G1), wh_ref, wl_ref)
    scatter = scatter_ref[...]
    for n in range(2):
        for k, block in enumerate(place(found[n])):
            out_ref[n, :, k * QW : (k + 1) * QW] = mm(scatter, block.astype(BF)).astype(BF)


def finish_kernel(wh_ref, wl_ref, left_ref, part_ref, coarse_ref, up_ref, down_ref):
    count = K * G2
    low_half = lax.broadcasted_iota(jnp.int32, (G2, 2 * CH), 1) < CH
    states = [[], []]
    for m in range(K):
        tiles = [[], []]
        for n in (2 * m, 2 * m + 1):
            first, second = coarse_ref[2 * n], coarse_ref[2 * n + 1]
            tiles[0].append(jnp.where(low_half, first, pltpu.roll(second, CH, 1)))
            tiles[1].append(jnp.where(low_half, pltpu.roll(first, CH, 1), second))
        for n in range(2):
            states[n].append(jnp.concatenate(tiles[n], axis=1))
    wide = times_filter(jnp.concatenate(states[0] + states[1], axis=0), wh_ref[...], wl_ref[...])
    for n, ref in enumerate((up_ref, down_ref)):
        rows = wide[n * count : (n + 1) * count]
        high, low = split(jnp.concatenate([rows[:, j * QW : (j + 1) * QW] for j in range(4)], axis=0))
        for k in range(K):
            lanes = slice(k * QW, (k + 1) * QW)
            left_high, left_low = left_ref[0, k], left_ref[1, k]
            found = mm(left_high, high) + mm(left_high, low) + mm(left_low, high)
            ref[:, lanes] = (part_ref[n, :, lanes] + found).astype(BF)
        ref.send()


def synthesize(states, scratch, rows, wh_ref, wl_ref):
    lefts = []
    for n in range(2):
        for band in range(2):
            for m in range(K):
                lanes = slice(m * QW, (m + 1) * QW)
                pair = [scratch[n, 1, rows, lanes], scratch[n, 2, rows, lanes]]
                if band == 0:
                    detail = scratch[n, 0, rows, lanes]
                    pair = [jnp.zeros_like(detail) if states is None else states[n][m], detail]
                lefts.append(jnp.concatenate(pair, axis=1))
    left = jnp.concatenate(lefts, axis=0).astype(BF)
    wide = mm(left, wh_ref[...]) + mm(left, wl_ref[...])
    count = rows.stop - rows.start
    out = []
    for n in range(2):
        parts = [[wide[((n * 2 + band) * K + m) * count :][:count] for m in range(K)] for band in range(2)]
        out.append(rows_inverse(parts))
    return out


def times_filter(left, high_filter, low_filter):
    high, low = split(left)
    return mm(high, high_filter) + mm(low, high_filter) + mm(high, low_filter)


def place(out):
    return [
        jnp.concatenate(
            [out[a][k][:, b * QW : (b + 1) * QW] for a in range(2) for b in range(2)], axis=0
        )
        for k in range(K)
    ]


def mode_tables(row_count, col_count):
    freqs = np.arange(MODES)
    angle = 2.0 * np.pi * np.outer(freqs, np.arange(row_count * H2)) / (row_count * H2)
    waves = np.stack([np.cos(angle), np.sin(angle)]).reshape(2, MODES, row_count, H2)
    rows = np.zeros((2, MODES, W2, row_count, G2))
    for i in range(H2):
        for j in range(W2):
            rows[:, :, j, :, i * W2 + j] = waves[:, :, :, i]
    rows = rows.reshape(2 * MODES * W2, row_count * G2)
    angle = 2.0 * np.pi * np.outer(freqs, np.arange(col_count * W2)) / (col_count * W2)
    cosine, sine = [part.reshape(MODES, col_count, W2) for part in (np.cos(angle), np.sin(angle))]
    places = np.zeros((col_count, 2, MODES, MODES, 2, MODES, W2))
    for u in range(MODES):
        for v in range(MODES):
            places[:, 0, u, v, 0, u] = cosine[v]
            places[:, 0, u, v, 1, u] = -sine[v]
            places[:, 1, u, v, 0, u] = sine[v]
            places[:, 1, u, v, 1, u] = cosine[v]
    places = places.reshape(col_count, 2 * MODES * MODES, 2 * MODES * W2)
    across = places.transpose(1, 0, 2).reshape(2 * MODES * MODES, -1)
    return [np.ascontiguousarray(part, np.float32) for part in (rows, rows.T, across, places.transpose(0, 2, 1))]


class Fetched:
    def __init__(self, source, scratch, sem):
        self.shape = scratch.shape
        self.ref = scratch
        self.copy = pltpu.make_async_copy(source, scratch, sem)
        self.copy.start()

    def arrived(self):
        if self.copy is not None:
            self.copy.wait()
            self.copy = None
        return self.ref

    def __getitem__(self, index):
        return self.arrived()[index]


class Returned:
    def __init__(self, target, scratch, sem):
        self.shape = scratch.shape
        self.ref = scratch
        self.copy = pltpu.make_async_copy(scratch, target, sem)
        self.started = False

    def __getitem__(self, index):
        return self.ref[index]

    def __setitem__(self, index, value):
        self.ref[index] = value

    def send(self):
        if not self.started:
            self.copy.start()
            self.started = True


def call(kernel, outs, ins, micros, smem=0, near=0, picks=None, near_out=False, scratch=(), limit=60):
    picks = picks or {}
    count, single = len(ins), not isinstance(outs, list)
    outs = [outs] if single else outs
    far = range(smem, count - near)
    blocks = [
        jax.eval_shape(lambda part, n=n: picks[n][0](part), ins[n]) if n in picks else ins[n] for n in far
    ]

    def wrapped(*refs):
        own = list(refs[:count])
        results = list(refs[count : count + len(outs)])
        rest = list(refs[count + len(outs) :])
        sems = rest.pop()
        for n, at in enumerate(far):
            source = picks[at][1](own[at], own[smem - 1]) if at in picks else own[at]
            own[at] = Fetched(source, rest.pop(0), sems.at[n])
        if not near_out:
            for n in range(len(outs)):
                results[n] = Returned(results[n], rest.pop(0), sems.at[len(far) + n])
        kernel(*own, *results, *rest)
        for operand in own:
            if isinstance(operand, Fetched):
                operand.arrived()
        if not near_out:
            for result in results:
                result.send()
            for result in results:
                result.copy.wait()

    where = [pltpu.SMEM] * smem + [pltpu.HBM] * len(far) + [pltpu.VMEM] * near
    inner = [pltpu.VMEM(block.shape, block.dtype) for block in blocks]
    if not near_out:
        inner += [pltpu.VMEM(out.shape, out.dtype) for out in outs]
    result = pl.pallas_call(
        wrapped,
        out_shape=outs,
        in_specs=[pl.BlockSpec(memory_space=space) for space in where],
        out_specs=[pl.BlockSpec(memory_space=pltpu.VMEM if near_out else pltpu.HBM) for _ in outs],
        scratch_shapes=inner + list(scratch) + [pltpu.SemaphoreType.DMA((len(far) + len(outs),))],
        compiler_params=pltpu.CompilerParams(vmem_limit_bytes=limit * 1024 * 1024),
        cost_estimate=pl.CostEstimate(
            flops=int(micros * 1.1e9), bytes_accessed=int(micros * 1e6), transcendentals=0
        ),
    )(*ins)
    return result[0] if single else result


def body(field, mix, stencil, spectral, cotangent):
    row_count, col_count = lax.axis_size("row"), lax.axis_size("col")
    wh, wl = [jnp.asarray(part) for part in halves(COL_FILTER)]
    wht, wlt = [jnp.asarray(np.ascontiguousarray(part.T)) for part in halves(COL_FILTER)]
    gather, scatter, send_side, send_ends, pick = [
        jnp.asarray(np.ascontiguousarray(part).astype(ml_dtypes.bfloat16))
        for part in (gather_table(), gather_table().T, SEND_SIDE, SEND_ENDS, PICK_BACK)
    ]
    rows, rows_back, across, places = [
        jnp.asarray(np.stack(halves(part), axis=part.ndim - 2))
        for part in mode_tables(row_count, col_count)
    ]
    place_here = jnp.stack([lax.axis_index("row"), lax.axis_index("col")])
    shape = jax.ShapeDtypeStruct

    def shift(message, dr, dc):
        axis, step = ("row", dr) if dr else ("col", dc)
        count = lax.axis_size(axis)
        return lax.ppermute(message, axis, [(n, (n - step) % count) for n in range(count)])

    def table(array):
        return jnp.asarray(np.ascontiguousarray(array))

    def high_low(array, axis):
        return table(np.concatenate(halves(array), axis=axis))

    coarse_filter = [table(part) for part in halves(COARSE_RIGHT)]
    coarse_back = [table(part.T) for part in halves(COARSE_RIGHT)]
    left_back = table(np.stack([part.transpose(0, 2, 1) for part in halves(COARSE_LEFT)]))
    field, cotangent = field.reshape(FI * FJ, F), cotangent.reshape(FI * FJ, F)
    part = call(
        coarse_kernel,
        shape((row_count, G2, 2 * CH), F32),
        (high_low(COARSE_LEFT, 1), *coarse_filter, field, cotangent),
        2,
        near_out=True,
    )
    part, field, cotangent = lax.optimization_barrier((part, field, cotangent))
    part = lax.all_to_all(part, "row", 0, 0, tiled=True)
    tile = 2 * CH
    loc, to_up, to_down, lead, lead_back, my_places, my_gains = call(
        analyze_kernel,
        [shape((LOC, 3 * F), BF)]
        + [shape((count, 3 * F), BF) for count in MSG_ROWS[:2]]
        + [shape((2 * QROWS, STACK_ROWS[0]), BF), shape((2 * INNER, QROWS), BF)]
        + [shape(places.shape[1:], BF), shape((2 * MODES * MODES, tile), F32)],
        (stencil.reshape(-1), place_here, field, cotangent, gather, wh, wl, send_side,
         jnp.asarray(TAP_AT), jnp.asarray(TAP_BACK), places, spectral.reshape(-1, F)),
        4,
        smem=2,
        picks={
            10: (lambda array: array[0], lambda ref, place: ref.at[place[1]]),
            11: (
                lambda array: array[:, :tile],
                lambda ref, place: ref.at[:, pl.ds(pl.multiple_of((place[0] // 2) * tile, tile), tile)],
            ),
        },
    )
    part = call(
        along_kernel,
        shape((col_count, 4 * MODES, tile), BF),
        (rows, part),
        1,
        near=2,
        near_out=True,
        limit=8,
    )
    part, to_up, to_down = lax.optimization_barrier((part, to_up, to_down))
    part = lax.all_to_all(part, "col", 0, 0, tiled=True)
    up, down = shift(to_up, *SIDES[0]), shift(to_down, *SIDES[1])
    to_left, to_right = call(
        ends_kernel,
        [shape((count, 3 * F), BF) for count in MSG_ROWS[2:]],
        (send_ends, loc, up, down),
        0.01,
    )
    left, right = shift(to_left, *SIDES[2]), shift(to_right, *SIDES[3])
    part = call(
        functools.partial(modes_kernel, 1.0 / math.sqrt(row_count * H2 * col_count * W2)),
        shape((row_count, G2, tile), F32),
        (across, my_places, rows_back, my_gains, part),
        1,
        near=5,
        near_out=True,
        limit=8,
    )
    part, loc = lax.optimization_barrier((part, loc))
    part = lax.all_to_all(part, "row", 0, 0, tiled=True)
    details = call(
        detail_kernel,
        shape((2, FI * FJ, F), BF),
        (lead, pick, loc, up, down, left, right, mix, lead_back, wht, wlt, scatter),
        7,
        scratch=[pltpu.VMEM((2, 3, INNER, F), F32)],
    )
    layer_out, grad_field = call(
        finish_kernel,
        [shape((FI * FJ, F), BF)] * 2,
        (*coarse_back, left_back, details, part),
        3,
        near=1,
    )
    return layer_out.reshape(FI, FJ, F), grad_field.reshape(FI, FJ, F)


def solution(mesh):
    placed = (P("row", "col", None), P(), P(), P(), P("row", "col", None))
    return jax.shard_map(
        body,
        mesh=mesh,
        in_specs=placed,
        out_specs=(P("row", "col", None), P("row", "col", None)),
        check_vma=False,
    )
```

time: 580 us -> 83 us (0.14); the launches traced: 571 us -> 82.2 us
  waiting for transfers between devices: 393 us -> 7.28 us
  matrix products: 39.9 us -> 0 us
  other arithmetic: 37.5 us -> 0.65 us
  local copies, waits for them, and re-layouts: 33 us -> 2.86 us
  Pallas kernels: 0 us -> 28.5 us
  between operations: 15 us -> 0.89 us
  starting transfers between devices: 52.1 us -> 42 us
    psum x1 -> x0, waiting for transfers between devices: 393 us -> none  [body(): modes = lax.psum(project(basis, state) * scale, ('row', 'col'))]
    ppermute x16 -> x4, starting transfers between devices: 52.1 us -> 11.2 us  [shift(): lax.ppermute(message, axis, [(n, (n - step) % count) for n in range(count)])]
    dot_general x24 -> x0, matrix products: 39.9 us -> none  [the longest x8 17.9 us: reconstruct(): jnp.einsum('xmak,ynbl,ijxymnc->iajbklc', filter_bank, filter_bank, parts,...]
    all_to_all x0 -> x3, starting transfers between devices: none -> 30.8 us  [the longest x1 16.5 us: body(): part = lax.all_to_all(part, 'col', 0, 0, tiled=True)]
    pallas_call x0 -> x7, Pallas kernels: none -> 28.5 us  [call(): pl.pallas_call(wrapped, out_shape=outs, in_specs=[pl.BlockSpec(memory_spa...]
    add x6 -> x0, other arithmetic: 27 us -> none  [the longest x4 27 us: apply_taps(): total = total + taps[shift_row + 1, shift_col + 1] * moved]
    reshape x13 -> x1, local copies, waits for them, and re-layouts: 16.1 us -> 0.59 us  [body(): stencil.reshape(-1)]
    slice x17 -> x0, local copies, waits for them, and re-layouts: 7.93 us -> none  [the longest x8 4.97 us: decompose(): return (parts[:, :, 0], parts[:, :, 1:])]
  transfers between devices with their start and end apart: 17 -> 7, of which waited for: 2 -> 3; matrix products, arithmetic and copies ran while one was open for 11% -> 2% of each run, Pallas kernels for 0% -> 23%
where the time goes in v1:
time: 83 us; the launch traced here: 82.2 us
  starting transfers between devices  42 us (51%)
  Pallas kernels  28.5 us (34%)
  waiting for transfers between devices  7.28 us (9%)
  local copies, waits for them, and re-layouts  2.86 us (3%)
  between operations  0.89 us (1%)
    pallas_call x7, Pallas kernels, call(): pl.pallas_call(wrapped, out_shape=outs, in_specs=[pl.BlockSpec(memory_spa...  28.5 us
    all_to_all x1, starting transfers between devices, body(): part = lax.all_to_all(part, 'col', 0, 0, tiled=True)  16.5 us
    all_to_all x2, starting transfers between devices, body(): part = lax.all_to_all(part, 'row', 0, 0, tiled=True)  14.2 us
    ppermute x4, starting transfers between devices, shift(): lax.ppermute(message, axis, [(n, (n - step) % count) for n in range(count)])  11.2 us
    all_to_all x1, waiting for transfers between devices, body(): part = lax.all_to_all(part, 'col', 0, 0, tiled=True)  4.6 us
    ppermute x4, waiting for transfers between devices, shift(): lax.ppermute(message, axis, [(n, (n - step) % count) for n in range(count)])  2.68 us
    unnamed x27, local copies, waits for them, and re-layouts  2.27 us
  transfers between devices with their start and end apart: 7, of which 3 were waited for; matrix products, arithmetic and copies ran while one was open for 2% of the time, Pallas kernels for 23%

profile of v1, /device:TPU:1, one launch (start us, length us, event | category | flops | bytes accessed | tf_op | source)
XLA Modules:
  0.0 82.2 jit_solution(7845021204148991668)
XLA Ops:
  0.6 4.2 %shard_map.257 = f32[16,16,128]{2,1,0:T(8,128)} custom-call(bf16[4,512,192]{2,1,0:T(8,128)(2,1)} %constant.69.clone.refs_0_, bf16[1024,256]{1,0:T(8,128)(2,1)} %constant.64.clone.refs_1_, bf16[1024,256]{1,0:T(8,128)(2,1)} %constant.65.clone.refs_2_, bf16[192,1024]{1,0:T(8,128)(2,1)} %bitcast.8, bf16[192,1024]{1,0:T(8,128)(2,1)} %bitcast.10), custom_call_target="tpu_custom_call" | custom-call | flops 2200000000 | bytes 2000000 | tf_op jit(solution)/shard_map/pallas_call | solution.py:582
  4.8 7.6 %all-to-all-start = ((f32[16,16,128]{2,1,0:T(8,128)}), f32[16,16,128]{2,1,0:T(8,128)S(1)}, u32[]{:S(2)}, u32[]{:S(2)}) async-start(f32[16,16,128]{2,1,0:T(8,128)} %shard_map.257), calls=%async_computation | async-start | bytes 262144 | tf_op jit(solution)/shard_map/all_to_all | solution.py:634
  12.4 0.6 reshape.22.refs_0_
  13.0 0.6 pad_add_fusion.refs_1_
  13.7 6.2 %shard_map.258 = (bf16[160,3072]{1,0:T(8,128)(2,1)}, bf16[24,3072]{1,0:T(8,128)(2,1)}, bf16[24,3072]{1,0:T(8,128)(2,1)}, bf16[288,224]{1,0:T(8,128)(2,1)}, bf16[...) custom-call(f32[18]{0:T(128)} %reshape.22.refs_0_, s32[2]{0:T(128)} %pad_add_fusion.refs_1_, ...), custom_call_target="tpu_custom_call" | custom-call | flops 4400000000 | bytes 4000000 | tf_op jit(solution)/shard_map/pallas_call | solution.py:582
  19.9 0.0 copy-start
  19.9 0.0 copy-start.1
  19.9 0.9 %shard_map.259 = bf16[32,32,128]{2,1,0:T(8,128)(2,1)} custom-call(bf16[2,32,256]{2,1,0:T(8,128)(2,1)S(1)} %copy-done.2, f32[16,16,128]{2,1,0:T(8,128)S(1)} %all-to-all-done.refs_1_), custom_call_target="tpu_custom_call" | custom-call | flops 1100000000 | bytes 1000000 | tf_op jit(solution)/shard_map/pallas_call | solution.py:582
  20.8 16.5 %all-to-all-start.1 = ((bf16[32,32,128]{2,1,0:T(8,128)(2,1)}), bf16[32,32,128]{2,1,0:T(8,128)(2,1)S(1)}, u32[]{:S(2)}, u32[]{:S(2)}) async-start(bf16[32,32,128]{2,1,0:T(8,128)(2,1)} %shard_map.259), calls=%async_computation.1 | async-start | bytes 524288 | tf_op jit(solution)/shard_map/all_to_all | solution.py:664
  37.4 3.2 %collective-permute-start = (bf16[24,3072]{1,0:T(8,128)(2,1)S(1)}, bf16[24,3072]{1,0:T(8,128)(2,1)S(1)}, u32[]{:S(2)}, u32[]{:S(2)}) collective-permute-start(bf16[24,3072]{1,0:T(8,128)(2,1)S(1)} %copy-done.12), channel_id=1, source_target_pairs={{0,32},{32,64},{64,96},{96,128},{128,160},{160,192},{192,224},{224... | collective-permute-start | bytes 442376 | tf_op jit(solution)/shard_map/ppermute | solution.py:614
  40.6 5.4 %collective-permute-start.1 = (bf16[24,3072]{1,0:T(8,128)(2,1)S(1)}, bf16[24,3072]{1,0:T(8,128)(2,1)S(1)}, u32[]{:S(2)}, u32[]{:S(2)}) collective-permute-start(bf16[24,3072]{1,0:T(8,128)(2,1)S(1)} %copy-done.11), channel_id=1, source_target_pairs={{0,480},{32,0},{64,32},{96,64},{128,96},{160,128},{192,160},{224,1... | collective-permute-start | bytes 442376 | tf_op jit(solution)/shard_map/ppermute | solution.py:614
  46.0 1.8 %collective-permute-done.refs_2_.refs_3_ = bf16[24,3072]{1,0:T(8,128)(2,1)S(1)} collective-permute-done((bf16[24,3072]{1,0:T(8,128)(2,1)S(1)}, bf16[24,3072]{1,0:T(8,128)(2,1)S(1)}, u32[]{:S(2)}, u32[]{:S(2)}) %collective-permute-start) | collective-permute-done | bytes 147488 | tf_op jit(solution)/shard_map/ppermute | solution.py:614
  47.8 0.9 %collective-permute-done.1.refs_3_.refs_4_ = bf16[24,3072]{1,0:T(8,128)(2,1)S(1)} collective-permute-done((bf16[24,3072]{1,0:T(8,128)(2,1)S(1)}, bf16[24,3072]{1,0:T(8,128)(2,1)S(1)}, u32[]{:S(2)}, u32[]{:S(2)}) %collective-permute-start.1) | collective-permute-done | bytes 147488 | tf_op jit(solution)/shard_map/ppermute | solution.py:614
  48.7 0.6 copy-done.6
  49.4 2.8 %shard_map.261 = (bf16[80,3072]{1,0:T(8,128)(2,1)}, bf16[80,3072]{1,0:T(8,128)(2,1)}) custom-call(bf16[160,208]{1,0:T(8,128)(2,1)} %constant.58.clone.refs_0_, bf16[160,3072]{1,0:T(8,128)(2,1)} %get-tuple-element.31.refs_1_.refs_2_, bf16[24,3072]{1,0:T(8,128)(2,1)} %copy-done.5, bf16[24,3072]{1,0:T(8,128)(2,1)} %copy-done.6), custom_call_target="tpu_custom_call" | custom-call | flops 11000000 | bytes 10000 | tf_op jit(solution)/shard_map/pallas_call | solution.py:582
  52.1 2.6 %collective-permute-start.2 = (bf16[80,3072]{1,0:T(8,128)(2,1)}, bf16[80,3072]{1,0:T(8,128)(2,1)S(1)}, u32[]{:S(2)}, u32[]{:S(2)}) collective-permute-start(bf16[80,3072]{1,0:T(8,128)(2,1)} %get-tuple-element.34), channel_id=1, source_target_pairs={{0,1},{1,2},{2,3},{3,4},{4,5},{5,6},{6,7},{7,8},{8,9},{9,10},{10,1... | collective-permute-start | bytes 1474568 | tf_op jit(solution)/shard_map/ppermute | solution.py:614
  54.8 4.6 %all-to-all-done.1.refs_4_ = bf16[32,32,128]{2,1,0:T(8,128)(2,1)S(1)} async-done(((bf16[32,32,128]{2,1,0:T(8,128)(2,1)}), bf16[32,32,128]{2,1,0:T(8,128)(2,1)S(1)}, u32[]{:S(2)}, u32[]{:S(2)}) %all-to-all-start.1) | async-done | bytes 262176 | tf_op jit(solution)/shard_map/all_to_all | solution.py:664
  59.4 1.4 %shard_map.260 = f32[16,16,128]{2,1,0:T(8,128)} custom-call(bf16[2,128,1024]{2,1,0:T(8,128)(2,1)S(1)} %copy-done, bf16[2,32,128]{2,1,0:T(8,128)(2,1)S(1)} %copy-done.4, bf16[2,256,32]{2,1,0:T(8,128)(2,1)S(1)} %copy-done.1, f32[128,128]{1,0:T(8,128)S(1)} %copy-done.3, bf16[32,32,128]{2,1,0:T(8,128)(2,1)S(1)} %all-to-all-done.1.refs_4_), custom_call_target="tpu_custom_call" | custom-call | flops 1100000000 | bytes 1000000 | tf_op jit(solution)/shard_map/pallas_call | solution.py:582
  60.8 6.6 %all-to-all-start.2 = ((f32[16,16,128]{2,1,0:T(8,128)}), f32[16,16,128]{2,1,0:T(8,128)S(1)}, u32[]{:S(2)}, u32[]{:S(2)}) async-start(f32[16,16,128]{2,1,0:T(8,128)} %shard_map.260), calls=%async_computation.2 | async-start | bytes 262144 | tf_op jit(solution)/shard_map/all_to_all | solution.py:683
  67.5 0.8 copy-done.9
  68.2 0.2 copy-done.10
  68.4 8.8 %shard_map.262.refs_3_ = bf16[2,192,1024]{2,1,0:T(8,128)(2,1)} custom-call(bf16[288,224]{1,0:T(8,128)(2,1)} %get-tuple-element.23.refs_0_, bf16[144,144]{1,0:T(8,128)(2,1)} %constant.59.clone.refs_1_, bf16[160,3072]{1,0:T(8,128)(2,1)} %get-tuple-element.31.refs_1_.refs_2_, bf16[24,3072]{1,0:T(8,128)(2,1)} %copy-done.5, bf16[24,3072]{1,0:T(8,128)(2,1)} %copy-done.6, ...), custom_call_target="tpu_custom_call" | custom-call | flops 7699999744 | bytes 7000000 | tf_op jit(solution)/shard_map/pallas_call | solution.py:582
  77.2 0.6 copy-done.7
  77.8 4.4 %shard_map.263 = (bf16[192,1024]{1,0:T(8,128)(2,1)}, bf16[192,1024]{1,0:T(8,128)(2,1)}) custom-call(bf16[256,1024]{1,0:T(8,128)(2,1)} %constant.66.clone.refs_0_, bf16[256,1024]{1,0:T(8,128)(2,1)} %constant.67.clone.refs_1_, bf16[2,4,192,256]{3,2,1,0:T(8,128)(2,1)} %constant.68.clone.refs_2_, bf16[2,192,1024]{2,1,0:T(8,128)(2,1)} %shard_map.262.refs_3_, ...), custom_call_target="tpu_custom_call" | custom-call | flops 3300000000 | bytes 3000000 | tf_op jit(solution)/shard_map/pallas_call | solution.py:582
  (26 shorter events, 0.1 us)
Async XLA Ops:
  0.6 11.8 %copy-start.8 = (f32[2,3,3]{2,0,1:T(2,128)S(1)}, f32[2,3,3]{2,0,1:T(2,128)}, u32[]{:S(2)}) copy-start(f32[2,3,3]{2,0,1:T(2,128)} %param.28) | copy-start | bytes 220
  4.8 15.1 %all-to-all-start = ((f32[16,16,128]{2,1,0:T(8,128)}), f32[16,16,128]{2,1,0:T(8,128)S(1)}, u32[]{:S(2)}, u32[]{:S(2)}) async-start(f32[16,16,128]{2,1,0:T(8,128)} %shard_map.257), calls=%async_computation | async-start | bytes 262144 | tf_op jit(solution)/shard_map/all_to_all | solution.py:634
  13.7 6.3 %copy-start.2 = (bf16[2,32,256]{2,1,0:T(8,128)(2,1)S(1)}, bf16[2,32,256]{2,1,0:T(8,128)(2,1)}, u32[]{:S(2)}) copy-start(bf16[2,32,256]{2,1,0:T(8,128)(2,1)} %constant.60.clone.refs_0_) | copy-start | bytes 98308
  19.9 17.5 %copy-start.12 = (bf16[24,3072]{1,0:T(8,128)(2,1)S(1)}, bf16[24,3072]{1,0:T(8,128)(2,1)}, u32[]{:S(2)}) copy-start(bf16[24,3072]{1,0:T(8,128)(2,1)} %get-tuple-element.32) | copy-start | bytes 442372
  19.9 20.8 %copy-start.11 = (bf16[24,3072]{1,0:T(8,128)(2,1)S(1)}, bf16[24,3072]{1,0:T(8,128)(2,1)}, u32[]{:S(2)}) copy-start(bf16[24,3072]{1,0:T(8,128)(2,1)} %get-tuple-element.33) | copy-start | bytes 442372
  19.9 39.5 %copy-start = (bf16[2,128,1024]{2,1,0:T(8,128)(2,1)S(1)}, bf16[2,128,1024]{2,1,0:T(8,128)(2,1)}, u32[]{:S(2)}) copy-start(bf16[2,128,1024]{2,1,0:T(8,128)(2,1)} %constant.62.clone.refs_0_) | copy-start | bytes 1572868
  19.9 39.5 %copy-start.1 = (bf16[2,256,32]{2,1,0:T(8,128)(2,1)S(1)}, bf16[2,256,32]{2,1,0:T(8,128)(2,1)}, u32[]{:S(2)}) copy-start(bf16[2,256,32]{2,1,0:T(8,128)(2,1)} %constant.61.clone.refs_2_) | copy-start | bytes 98308
  19.9 39.5 %copy-start.3 = (f32[128,128]{1,0:T(8,128)S(1)}, f32[128,128]{1,0:T(8,128)}, u32[]{:S(2)}) copy-start(f32[128,128]{1,0:T(8,128)} %get-tuple-element.25.refs_3_) | copy-start | bytes 196612
  19.9 39.5 %copy-start.4 = (bf16[2,32,128]{2,1,0:T(8,128)(2,1)S(1)}, bf16[2,32,128]{2,1,0:T(8,128)(2,1)}, u32[]{:S(2)}) copy-start(bf16[2,32,128]{2,1,0:T(8,128)(2,1)} %get-tuple-element.24.refs_1_) | copy-start | bytes 49156
  20.8 38.5 %all-to-all-start.1 = ((bf16[32,32,128]{2,1,0:T(8,128)(2,1)}), bf16[32,32,128]{2,1,0:T(8,128)(2,1)S(1)}, u32[]{:S(2)}, u32[]{:S(2)}) async-start(bf16[32,32,128]{2,1,0:T(8,128)(2,1)} %shard_map.259), calls=%async_computation.1 | async-start | bytes 524288 | tf_op jit(solution)/shard_map/all_to_all | solution.py:664
  37.4 10.4 %collective-permute-start = (bf16[24,3072]{1,0:T(8,128)(2,1)S(1)}, bf16[24,3072]{1,0:T(8,128)(2,1)S(1)}, u32[]{:S(2)}, u32[]{:S(2)}) collective-permute-start(bf16[24,3072]{1,0:T(8,128)(2,1)S(1)} %copy-done.12), channel_id=1, source_target_pairs={{0,32},{32,64},{64,96},{96,128},{128,160},{160,192},{192,224},{224... | collective-permute-start | bytes 442376 | tf_op jit(solution)/shard_map/ppermute | solution.py:614
  40.6 8.1 %collective-permute-start.1 = (bf16[24,3072]{1,0:T(8,128)(2,1)S(1)}, bf16[24,3072]{1,0:T(8,128)(2,1)S(1)}, u32[]{:S(2)}, u32[]{:S(2)}) collective-permute-start(bf16[24,3072]{1,0:T(8,128)(2,1)S(1)} %copy-done.11), channel_id=1, source_target_pairs={{0,480},{32,0},{64,32},{96,64},{128,96},{160,128},{192,160},{224,1... | collective-permute-start | bytes 442376 | tf_op jit(solution)/shard_map/ppermute | solution.py:614
  47.8 0.9 %copy-start.5 = (bf16[24,3072]{1,0:T(8,128)(2,1)}, bf16[24,3072]{1,0:T(8,128)(2,1)S(1)}, u32[]{:S(2)}) copy-start(bf16[24,3072]{1,0:T(8,128)(2,1)S(1)} %collective-permute-done.refs_2_.refs_3_) | copy-start | bytes 442372
  48.7 0.7 copy-start.6
  52.1 15.3 %collective-permute-start.2 = (bf16[80,3072]{1,0:T(8,128)(2,1)}, bf16[80,3072]{1,0:T(8,128)(2,1)S(1)}, u32[]{:S(2)}, u32[]{:S(2)}) collective-permute-start(bf16[80,3072]{1,0:T(8,128)(2,1)} %get-tuple-element.34), channel_id=1, source_target_pairs={{0,1},{1,2},{2,3},{3,4},{4,5},{5,6},{6,7},{7,8},{8,9},{9,10},{10,1... | collective-permute-start | bytes 1474568 | tf_op jit(solution)/shard_map/ppermute | solution.py:614
  54.8 12.7 %collective-permute-start.3 = (bf16[80,3072]{1,0:T(8,128)(2,1)}, bf16[80,3072]{1,0:T(8,128)(2,1)S(1)}, u32[]{:S(2)}, u32[]{:S(2)}) collective-permute-start(bf16[80,3072]{1,0:T(8,128)(2,1)} %get-tuple-element.35), channel_id=1, source_target_pairs={{0,31},{1,0},{2,1},{3,2},{4,3},{5,4},{6,5},{7,6},{8,7},{9,8},{10,9... | collective-permute-start | bytes 1474568 | tf_op jit(solution)/shard_map/ppermute | solution.py:614
  60.8 16.4 %all-to-all-start.2 = ((f32[16,16,128]{2,1,0:T(8,128)}), f32[16,16,128]{2,1,0:T(8,128)S(1)}, u32[]{:S(2)}, u32[]{:S(2)}) async-start(f32[16,16,128]{2,1,0:T(8,128)} %shard_map.260), calls=%async_computation.2 | async-start | bytes 262144 | tf_op jit(solution)/shard_map/all_to_all | solution.py:683
  67.4 0.8 copy-start.9
  67.5 0.9 %copy-start.10 = (bf16[80,3072]{1,0:T(8,128)(2,1)}, bf16[80,3072]{1,0:T(8,128)(2,1)S(1)}, u32[]{:S(2)}) copy-start(bf16[80,3072]{1,0:T(8,128)(2,1)S(1)} %collective-permute-done.3.refs_6_) | copy-start | bytes 1474564
  77.2 0.6 copy-start.7

commit v2 on v1

--- a/solution.py
+++ b/solution.py
@@ -115,6 +115,8 @@
         COARSE_LEFT[:, j_ % 4, :, (i_ // 4) * W2 + j_ // 4, i_ * FJ + j_] = TWICE[:, i_ % 4, :].T
 COARSE_LEFT = COARSE_LEFT.reshape(K, 4 * K * G2, FI * FJ)
 COARSE_RIGHT = np.kron(TWICE.transpose(1, 2, 0).reshape(4 * K, K), np.eye(CH))
+SUB = 32
+TILE = 128
 
 
 def gather_table():
@@ -269,32 +271,39 @@
     return out
 
 
-def coarse_kernel(left_ref, wh_ref, wl_ref, field_ref, cot_ref, part_ref):
-    count = K * G2
-    found = []
-    for source in (field_ref, cot_ref):
-        total = None
-        for k in range(K):
-            term = mm(left_ref[k], source[:, k * QW : (k + 1) * QW])
-            total = term if total is None else total + term
-        found.append(total[: 4 * count] + total[4 * count :])
-    state = None
-    for j in range(4):
-        piece = jnp.concatenate([part[j * count : (j + 1) * count] for part in found], axis=0)
-        rows = slice(j * QW, (j + 1) * QW)
-        term = times_filter(piece, wh_ref[rows], wl_ref[rows])
-        state = term if state is None else state + term
-    low_half = lax.broadcasted_iota(jnp.int32, (G2, 2 * CH), 1) < CH
-    for m in range(K):
-        for half in range(2):
-            lanes = slice(half * 2 * CH, (half + 1) * 2 * CH)
-            first = state[m * G2 : (m + 1) * G2, lanes]
-            second = state[count + m * G2 : count + (m + 1) * G2, lanes]
-            part_ref[m * K + 2 * half] = jnp.where(low_half, first, pltpu.roll(second, CH, 1))
-            part_ref[m * K + 2 * half + 1] = jnp.where(low_half, pltpu.roll(first, CH, 1), second)
-
-
-def analyze_kernel(stencil_ref, place_ref, field_ref, cot_ref, gather_ref, wh_ref, wl_ref, send_ref, tap_ref, tap_back_ref, places_ref, gains_ref, loc_ref, up_ref, down_ref, lead_ref, lead_back_ref, my_places_ref, my_gains_ref):
+def quarter(index):
+    return lax.broadcasted_iota(jnp.int32, (8, TILE), 1) // SUB == index
+
+
+def pack_channels(first, second, out_ref):
+    for n in range(F // TILE):
+        lanes = slice(n * TILE, (n + 1) * TILE)
+        sources = [first[:8, lanes], second[:8, lanes], first[8:, lanes], second[8:, lanes]]
+        for s in range(TILE // SUB):
+            total = None
+            for t, source in enumerate(sources):
+                moved = source if s == t else pltpu.roll(source, (t - s) % 4 * SUB, 1)
+                total = moved if total is None else jnp.where(quarter(t), moved, total)
+            out_ref[n * 4 + s] = total
+
+
+def unpack_channels(ref):
+    out = [[], []]
+    for n in range(F // TILE):
+        sources = [ref[n * 4 + s] for s in range(TILE // SUB)]
+        found = []
+        for t in range(4):
+            total = None
+            for s, source in enumerate(sources):
+                moved = source if s == t else pltpu.roll(source, (s - t) % 4 * SUB, 1)
+                total = moved if total is None else jnp.where(quarter(s), moved, total)
+            found.append(total)
+        out[0].append(jnp.concatenate([found[0], found[2]], axis=0))
+        out[1].append(jnp.concatenate([found[1], found[3]], axis=0))
+    return out
+
+
+def analyze_kernel(field_ref, cot_ref, gather_ref, wh_ref, wl_ref, send_ref, loc_ref, up_ref, down_ref, part_ref):
     gather = gather_ref[...]
     lefts = [[], []]
     for source in (field_ref, cot_ref):
@@ -327,6 +336,7 @@
         rows = slice(b * QW, (b + 1) * QW)
         term = mm(high, wh_ref[rows]) + mm(low, wh_ref[rows]) + mm(high, wl_ref[rows])
         mixed = term if mixed is None else mixed + term
+    coarse = []
     for n in range(2):
         parts = [[mixed[((n * 2 + a) * K + k) * G2 :][:G2] for k in range(K)] for a in range(2)]
         out = rows_forward(parts)
@@ -335,44 +345,71 @@
         at = n * INNER
         loc_ref[at : at + G1, :] = locs[n]
         loc_ref[at + G1 : at + INNER, :] = jnp.concatenate(detail, axis=1).astype(BF)
+        coarse.append(jnp.concatenate([out[0][m][:, :QW] for m in range(K)], axis=1))
+    pack_channels(*coarse, part_ref)
+    part_ref.send()
+    loc_ref.send()
     moved = mm(send_ref[...], loc_ref[...])
     up_ref[...] = moved[: MSG_ROWS[0]].astype(BF)
     down_ref[...] = moved[MSG_ROWS[0] :].astype(BF)
-    up_ref.send()
-    down_ref.send()
-    loc_ref.send()
-    taps = [stencil_ref[n] for n in range(18)]
+
+
+def stack(parts):
+    return jnp.concatenate([part.astype(F32) for part in parts], axis=0).astype(BF)
+
+
+def along_kernel(rows_ref, parts_ref, out_ref):
+    high, low = split(parts_ref[...].reshape(-1, TILE))
+
+    def times(n):
+        left_high = rows_ref[n, 0]
+        return mm(left_high, high) + mm(rows_ref[n, 1], high) + mm(left_high, low)
+
+    near = lax.broadcasted_iota(jnp.int32, (4 * MODES, TILE), 1) < TILE // 2
+    first = times(0) + pltpu.roll(times(1), TILE // 2, 1)
+    second = pltpu.roll(times(2), TILE // 2, 1) + times(3)
+    out = jnp.where(near, first, second).astype(BF)
+    for n in range(out_ref.shape[0]):
+        out_ref[n] = out
+
+
+def ends_kernel(stencil_ref, send_ref, loc_ref, up_ref, down_ref, tap_ref, tap_back_ref, places_ref, gains_ref, left_ref, right_ref, lead_ref, lead_back_ref, my_places_ref, my_gains_ref):
+    known = jnp.concatenate([loc_ref[...], stack([up_ref[...], down_ref[...]])], axis=0)
+    moved = mm(send_ref[...], known).astype(BF)
+    left_ref[...] = moved[: MSG_ROWS[2]]
+    left_ref.send()
+    right_ref[...] = moved[MSG_ROWS[2] :]
+    right_ref.send()
+    taps = [stencil_ref[n // 9, n // 3 % 3, n % 3] for n in range(18)]
     lead_ref[:QROWS], lead_ref[QROWS:] = split(tap_matrix(tap_ref[...], taps))
     lead_back_ref[:INNER], lead_back_ref[INNER:] = split(tap_matrix(tap_back_ref[...], taps))
     my_places_ref[...] = places_ref[...]
     gains = gains_ref[...]
-    low_half = lax.broadcasted_iota(jnp.int32, gains.shape, 1) < CH
-    even = (place_ref[0] % 2) == 0
-    my_gains_ref[...] = jnp.where(low_half == even, gains, pltpu.roll(gains, CH, 1))
-
-
-def stack(parts):
-    return jnp.concatenate([part.astype(F32) for part in parts], axis=0).astype(BF)
-
-
-def along_kernel(rows_ref, parts_ref, out_ref):
-    out = mm3(rows_ref, parts_ref[...].reshape(-1, 2 * CH)).astype(BF)
-    for n in range(out_ref.shape[0]):
-        out_ref[n] = out
-
-
-def ends_kernel(send_ref, loc_ref, up_ref, down_ref, left_ref, right_ref):
-    known = jnp.concatenate([loc_ref[...], stack([up_ref[...], down_ref[...]])], axis=0)
-    moved = mm(send_ref[...], known).astype(BF)
-    left_ref[...] = moved[: MSG_ROWS[2]]
-    right_ref[...] = moved[MSG_ROWS[2] :]
+    own = (lax.axis_index("row") * 2 + lax.axis_index("col") % 2) % 4
+    group = lax.broadcasted_iota(jnp.int32, gains.shape, 1) // SUB
+    total = jnp.zeros_like(gains)
+    for s in range(4):
+        for t in range(2):
+            moved = pltpu.roll(gains, (t - s) % 4 * SUB, 1) if s != t else gains
+            total = jnp.where((group == t) & (own == s), moved, total)
+    my_gains_ref[...] = total
 
 
 def modes_kernel(scale, across_ref, table_ref, rows_ref, gains_ref, parts_ref, out_ref):
-    parts = parts_ref[...].reshape(-1, 2 * CH)
-    modes = mm(across_ref[0], parts) + mm(across_ref[1], parts)
-    wide = mm3(table_ref, gains_ref[...] * modes * scale)
-    out_ref[...] = mm3(rows_ref, wide).reshape(out_ref.shape)
+    parts = parts_ref[...].reshape(-1, TILE)
+    half = TILE // 2
+    modes = mm(across_ref[0, 0], parts) + mm(across_ref[0, 1], parts)
+    modes = modes + pltpu.roll(mm(across_ref[1, 0], parts) + mm(across_ref[1, 1], parts), half, 1)
+    coeffs = gains_ref[...] * modes * scale
+    near = lax.broadcasted_iota(jnp.int32, (4 * MODES, TILE), 1) < half
+    wide = jnp.where(
+        near, mm3(table_ref.at[0], coeffs), pltpu.roll(mm3(table_ref.at[1], coeffs), half, 1)
+    )
+    first, second = mm3(rows_ref.at[0], wide), mm3(rows_ref.at[1], wide)
+    near = lax.broadcasted_iota(jnp.int32, first.shape, 1) < half
+    shape = (out_ref.shape[0], 8, TILE)
+    out_ref[:, 0] = jnp.where(near, first, pltpu.roll(second, half, 1)).reshape(shape)
+    out_ref[:, 1] = jnp.where(near, pltpu.roll(first, half, 1), second).reshape(shape)
 
 
 def mm3(left_ref, right):
@@ -415,12 +452,12 @@
         jnp.concatenate(backs, axis=0), mix, (((1,), (1,)), ((), ())), preferred_element_type=F32
     )
     for band in range(3):
-        scratch[0, band] = mixed[band * INNER : (band + 1) * INNER]
+        scratch[0, band] = mixed[band * INNER : (band + 1) * INNER].astype(BF)
         grad = (back[band * QROWS : (band + 1) * QROWS] * derivatives[band]).astype(BF)
         found = mm(lead_back, grad)
-        scratch[1, band] = found[:INNER] + found[INNER:]
+        scratch[1, band] = (found[:INNER] + found[INNER:]).astype(BF)
     found = synthesize(None, scratch, slice(G1, INNER), wh_ref, wl_ref)
-    found = synthesize([place(out) for out in found], scratch, slice(0, G1), wh_ref, wl_ref)
+    found = synthesize([[part.astype(BF) for part in place(out)] for out in found], scratch, slice(0, G1), wh_ref, wl_ref)
     scatter = scatter_ref[...]
     for n in range(2):
         for k, block in enumerate(place(found[n])):
@@ -429,16 +466,10 @@
 
 def finish_kernel(wh_ref, wl_ref, left_ref, part_ref, coarse_ref, up_ref, down_ref):
     count = K * G2
-    low_half = lax.broadcasted_iota(jnp.int32, (G2, 2 * CH), 1) < CH
-    states = [[], []]
-    for m in range(K):
-        tiles = [[], []]
-        for n in (2 * m, 2 * m + 1):
-            first, second = coarse_ref[2 * n], coarse_ref[2 * n + 1]
-            tiles[0].append(jnp.where(low_half, first, pltpu.roll(second, CH, 1)))
-            tiles[1].append(jnp.where(low_half, pltpu.roll(first, CH, 1), second))
-        for n in range(2):
-            states[n].append(jnp.concatenate(tiles[n], axis=1))
+    tiles = unpack_channels(coarse_ref)
+    states = [
+        [jnp.concatenate(own[2 * m : 2 * m + 2], axis=1) for m in range(K)] for own in tiles
+    ]
     wide = times_filter(jnp.concatenate(states[0] + states[1], axis=0), wh_ref[...], wl_ref[...])
     for n, ref in enumerate((up_ref, down_ref)):
         rows = wide[n * count : (n + 1) * count]
@@ -462,7 +493,7 @@
                     detail = scratch[n, 0, rows, lanes]
                     pair = [jnp.zeros_like(detail) if states is None else states[n][m], detail]
                 lefts.append(jnp.concatenate(pair, axis=1))
-    left = jnp.concatenate(lefts, axis=0).astype(BF)
+    left = jnp.concatenate(lefts, axis=0)
     wide = mm(left, wh_ref[...]) + mm(left, wl_ref[...])
     count = rows.stop - rows.start
     out = []
@@ -486,7 +517,7 @@
     ]
 
 
-def mode_tables(row_count, col_count):
+def mode_tables(row_count, chip_count):
     freqs = np.arange(MODES)
     angle = 2.0 * np.pi * np.outer(freqs, np.arange(row_count * H2)) / (row_count * H2)
     waves = np.stack([np.cos(angle), np.sin(angle)]).reshape(2, MODES, row_count, H2)
@@ -494,19 +525,26 @@
     for i in range(H2):
         for j in range(W2):
             rows[:, :, j, :, i * W2 + j] = waves[:, :, :, i]
-    rows = rows.reshape(2 * MODES * W2, row_count * G2)
-    angle = 2.0 * np.pi * np.outer(freqs, np.arange(col_count * W2)) / (col_count * W2)
-    cosine, sine = [part.reshape(MODES, col_count, W2) for part in (np.cos(angle), np.sin(angle))]
-    places = np.zeros((col_count, 2, MODES, MODES, 2, MODES, W2))
+    rows = rows.reshape(2 * MODES * W2, row_count, 2, 8)
+    back = rows.transpose(2, 1, 3, 0).reshape(2, row_count * 8, -1)
+    along = np.zeros((2, 2, 2 * MODES * W2, row_count, 2, 8))
+    for core in range(2):
+        for half in range(2):
+            along[core, half, :, :, core] = rows[:, :, half]
+    along = along.reshape(4, 2 * MODES * W2, -1)
+    angle = 2.0 * np.pi * np.outer(freqs, np.arange(chip_count * 2 * W2)) / (chip_count * 2 * W2)
+    cosine, sine = [part.reshape(MODES, chip_count, 2, W2) for part in (np.cos(angle), np.sin(angle))]
+    places = np.zeros((chip_count, 2, 2, MODES, MODES, 2, MODES, W2))
     for u in range(MODES):
         for v in range(MODES):
-            places[:, 0, u, v, 0, u] = cosine[v]
-            places[:, 0, u, v, 1, u] = -sine[v]
-            places[:, 1, u, v, 0, u] = sine[v]
-            places[:, 1, u, v, 1, u] = cosine[v]
-    places = places.reshape(col_count, 2 * MODES * MODES, 2 * MODES * W2)
-    across = places.transpose(1, 0, 2).reshape(2 * MODES * MODES, -1)
-    return [np.ascontiguousarray(part, np.float32) for part in (rows, rows.T, across, places.transpose(0, 2, 1))]
+            places[:, :, 0, u, v, 0, u] = cosine[v]
+            places[:, :, 0, u, v, 1, u] = -sine[v]
+            places[:, :, 1, u, v, 0, u] = sine[v]
+            places[:, :, 1, u, v, 1, u] = cosine[v]
+    places = places.reshape(chip_count, 2, 2 * MODES * MODES, 2 * MODES * W2)
+    across = places.transpose(1, 2, 0, 3).reshape(2, 2 * MODES * MODES, -1)
+    places = places.transpose(0, 1, 3, 2)
+    return [jnp.asarray(np.stack(halves(part), axis=part.ndim - 2)) for part in (along, back, across, places)]
 
 
 class Fetched:
@@ -560,7 +598,7 @@
         rest = list(refs[count + len(outs) :])
         sems = rest.pop()
         for n, at in enumerate(far):
-            source = picks[at][1](own[at], own[smem - 1]) if at in picks else own[at]
+            source = picks[at][1](own[at]) if at in picks else own[at]
             own[at] = Fetched(source, rest.pop(0), sems.at[n])
         if not near_out:
             for n in range(len(outs)):
@@ -601,92 +639,85 @@
         jnp.asarray(np.ascontiguousarray(part).astype(ml_dtypes.bfloat16))
         for part in (gather_table(), gather_table().T, SEND_SIDE, SEND_ENDS, PICK_BACK)
     ]
-    rows, rows_back, across, places = [
-        jnp.asarray(np.stack(halves(part), axis=part.ndim - 2))
-        for part in mode_tables(row_count, col_count)
-    ]
-    place_here = jnp.stack([lax.axis_index("row"), lax.axis_index("col")])
+    chip_count = col_count // 2
+    along, back, across, places = mode_tables(row_count, chip_count)
     shape = jax.ShapeDtypeStruct
+
+    def table(array):
+        return jnp.asarray(np.ascontiguousarray(array))
 
     def shift(message, dr, dc):
         axis, step = ("row", dr) if dr else ("col", dc)
         count = lax.axis_size(axis)
         return lax.ppermute(message, axis, [(n, (n - step) % count) for n in range(count)])
 
-    def table(array):
-        return jnp.asarray(np.ascontiguousarray(array))
-
-    def high_low(array, axis):
-        return table(np.concatenate(halves(array), axis=axis))
-
-    coarse_filter = [table(part) for part in halves(COARSE_RIGHT)]
     coarse_back = [table(part.T) for part in halves(COARSE_RIGHT)]
     left_back = table(np.stack([part.transpose(0, 2, 1) for part in halves(COARSE_LEFT)]))
-    field, cotangent = field.reshape(FI * FJ, F), cotangent.reshape(FI * FJ, F)
-    part = call(
-        coarse_kernel,
-        shape((row_count, G2, 2 * CH), F32),
-        (high_low(COARSE_LEFT, 1), *coarse_filter, field, cotangent),
-        2,
-        near_out=True,
-    )
-    part, field, cotangent = lax.optimization_barrier((part, field, cotangent))
-    part = lax.all_to_all(part, "row", 0, 0, tiled=True)
-    tile = 2 * CH
-    loc, to_up, to_down, lead, lead_back, my_places, my_gains = call(
+    plane = [
+        [r * col_count + 2 * z + core for r in range(row_count) for core in range(2)]
+        for z in range(chip_count)
+    ]
+    chips = [[2 * z + core for z in range(chip_count)] for core in range(2)]
+
+    def over_plane(pieces):
+        return lax.all_to_all(pieces, ("row", "col"), 0, 0, tiled=True, axis_index_groups=plane)
+
+    loc, to_up, to_down, part = call(
         analyze_kernel,
         [shape((LOC, 3 * F), BF)]
         + [shape((count, 3 * F), BF) for count in MSG_ROWS[:2]]
-        + [shape((2 * QROWS, STACK_ROWS[0]), BF), shape((2 * INNER, QROWS), BF)]
-        + [shape(places.shape[1:], BF), shape((2 * MODES * MODES, tile), F32)],
-        (stencil.reshape(-1), place_here, field, cotangent, gather, wh, wl, send_side,
-         jnp.asarray(TAP_AT), jnp.asarray(TAP_BACK), places, spectral.reshape(-1, F)),
+        + [shape((2 * row_count, 8, TILE), F32)],
+        (field.reshape(FI * FJ, F), cotangent.reshape(FI * FJ, F), gather, wh, wl, send_side),
         4,
-        smem=2,
-        picks={
-            10: (lambda array: array[0], lambda ref, place: ref.at[place[1]]),
-            11: (
-                lambda array: array[:, :tile],
-                lambda ref, place: ref.at[:, pl.ds(pl.multiple_of((place[0] // 2) * tile, tile), tile)],
-            ),
-        },
-    )
+    )
+    part = over_plane(part)
+    up, down = shift(to_up, *SIDES[0]), shift(to_down, *SIDES[1])
     part = call(
         along_kernel,
-        shape((col_count, 4 * MODES, tile), BF),
-        (rows, part),
+        shape((chip_count, 4 * MODES, TILE), BF),
+        (along, part),
         1,
         near=2,
         near_out=True,
         limit=8,
     )
-    part, to_up, to_down = lax.optimization_barrier((part, to_up, to_down))
-    part = lax.all_to_all(part, "col", 0, 0, tiled=True)
-    up, down = shift(to_up, *SIDES[0]), shift(to_down, *SIDES[1])
-    to_left, to_right = call(
+    part, loc = lax.optimization_barrier((part, loc))
+    part = lax.all_to_all(part, "col", 0, 0, tiled=True, axis_index_groups=chips)
+    to_left, to_right, lead, lead_back, my_places, my_gains = call(
         ends_kernel,
-        [shape((count, 3 * F), BF) for count in MSG_ROWS[2:]],
-        (send_ends, loc, up, down),
+        [shape((count, 3 * F), BF) for count in MSG_ROWS[2:]]
+        + [shape((2 * QROWS, STACK_ROWS[0]), BF), shape((2 * INNER, QROWS), BF)]
+        + [shape(places.shape[1:], BF), shape((2 * MODES * MODES, TILE), F32)],
+        (stencil, send_ends, loc, up, down, jnp.asarray(TAP_AT), jnp.asarray(TAP_BACK), places,
+         spectral.reshape(-1, F)),
         0.01,
+        smem=1,
+        picks={
+            7: (lambda array: array[0], lambda ref: ref.at[lax.axis_index("col") // 2]),
+            8: (
+                lambda array: array[:, :TILE],
+                lambda ref: ref.at[:, pl.ds(pl.multiple_of(lax.axis_index("row") // 2 * TILE, TILE), TILE)],
+            ),
+        },
     )
     left, right = shift(to_left, *SIDES[2]), shift(to_right, *SIDES[3])
     part = call(
         functools.partial(modes_kernel, 1.0 / math.sqrt(row_count * H2 * col_count * W2)),
-        shape((row_count, G2, tile), F32),
-        (across, my_places, rows_back, my_gains, part),
+        shape((row_count, 2, 8, TILE), F32),
+        (across, my_places, back, my_gains, part),
         1,
         near=5,
         near_out=True,
         limit=8,
     )
     part, loc = lax.optimization_barrier((part, loc))
-    part = lax.all_to_all(part, "row", 0, 0, tiled=True)
+    part = over_plane(part.reshape(2 * row_count, 8, TILE))
     details = call(
         detail_kernel,
         shape((2, FI * FJ, F), BF),
         (lead, pick, loc, up, down, left, right, mix, lead_back, wht, wlt, scatter),
         7,
-        scratch=[pltpu.VMEM((2, 3, INNER, F), F32)],
+        scratch=[pltpu.VMEM((2, 3, INNER, F), BF)],
     )
     layer_out, grad_field = call(
         finish_kernel,

time: 83 us -> 76.9 us (0.927)
  Pallas kernels: 28.5 us -> 24.5 us
  waiting for transfers between devices: 7.28 us -> 4.36 us
  local copies, waits for them, and re-layouts: 2.86 us -> 4.49 us
    pallas_call x7 -> x6, Pallas kernels: 28.5 us -> 24.5 us  [call(): pl.pallas_call(wrapped, out_shape=outs, in_specs=[pl.BlockSpec(memory_spa...]
    ppermute x4, waiting for transfers between devices: 2.68 us -> 0.01 us  [shift(): lax.ppermute(message, axis, [(n, (n - step) % count) for n in range(count)])]
    unnamed x27 -> x23, local copies, waits for them, and re-layouts: 2.27 us -> 4.49 us
  transfers between devices with their start and end apart: 7 -> 7, of which waited for: 3 -> 1; matrix products, arithmetic and copies ran while one was open for 2% -> 1% of each run, Pallas kernels for 23% -> 20%
where the time goes in v2:
time: 76.9 us; the launch traced here: 76.3 us
  starting transfers between devices  42.1 us (55%)
  Pallas kernels  24.5 us (32%)
  local copies, waits for them, and re-layouts  4.49 us (6%)
  waiting for transfers between devices  4.36 us (6%)
  between operations  0.83 us (1%)
    pallas_call x6, Pallas kernels, call(): pl.pallas_call(wrapped, out_shape=outs, in_specs=[pl.BlockSpec(memory_spa...  24.5 us
    all_to_all x2, starting transfers between devices, over_plane(): lax.all_to_all(pieces, ('row', 'col'), 0, 0, tiled=True, axis_index_group...  17.6 us
    all_to_all x1, starting transfers between devices, body(): lax.all_to_all(part, 'col', 0, 0, tiled=True, axis_index_groups=chips)  13.2 us
    ppermute x4, starting transfers between devices, shift(): lax.ppermute(message, axis, [(n, (n - step) % count) for n in range(count)])  11.3 us
    unnamed x23, local copies, waits for them, and re-layouts  4.49 us
    all_to_all x1, waiting for transfers between devices, body(): lax.all_to_all(part, 'col', 0, 0, tiled=True, axis_index_groups=chips)  4.35 us
  transfers between devices with their start and end apart: 7, of which 1 were waited for; matrix products, arithmetic and copies ran while one was open for 1% of the time, Pallas kernels for 20%

profile of v2, /device:TPU:1, one launch (start us, length us, event | category | flops | bytes accessed | tf_op | source)
XLA Modules:
  0.0 76.3 jit_solution(3422246474466782972)
XLA Ops:
  0.6 0.0 copy-start.4
  0.6 5.1 %shard_map.230 = (bf16[160,3072]{1,0:T(8,128)(2,1)}, bf16[24,3072]{1,0:T(8,128)(2,1)}, bf16[24,3072]{1,0:T(8,128)(2,1)}, f32[32,8,128]{2,1,0:T(8,128)}) custom-call(bf16[192,1024]{1,0:T(8,128)(2,1)} %bitcast.7, bf16[192,1024]{1,0:T(8,128)(2,1)} %bitcast.8, bf16[256,192]{1,0:T(8,128)(2,1)} %constant.40.clone.refs_2_, ...), custom_call_target="tpu_custom_call" | custom-call | flops 4400000000 | bytes 4000000 | tf_op jit(solution)/shard_map/pallas_call | solution.py:620
  5.8 10.4 %all-to-all-start = ((f32[32,8,128]{2,1,0:T(8,128)}), f32[32,8,128]{2,1,0:T(8,128)S(1)}, u32[]{:S(2)}, u32[]{:S(2)}) async-start(f32[32,8,128]{2,1,0:T(8,128)} %get-tuple-element.18), calls=%async_computation | async-start | bytes 262144 | tf_op jit(solution)/shard_map/all_to_all | solution.py:663
  16.2 3.3 %collective-permute-start = (bf16[24,3072]{1,0:T(8,128)(2,1)}, bf16[24,3072]{1,0:T(8,128)(2,1)S(1)}, u32[]{:S(2)}, u32[]{:S(2)}) collective-permute-start(bf16[24,3072]{1,0:T(8,128)(2,1)} %get-tuple-element.21), channel_id=1, source_target_pairs={{0,32},{32,64},{64,96},{96,128},{128,160},{160,192},{192,224},{224... | collective-permute-start | bytes 442376 | tf_op jit(solution)/shard_map/ppermute | solution.py:652
  19.5 5.4 %collective-permute-start.1 = (bf16[24,3072]{1,0:T(8,128)(2,1)}, bf16[24,3072]{1,0:T(8,128)(2,1)S(1)}, u32[]{:S(2)}, u32[]{:S(2)}) collective-permute-start(bf16[24,3072]{1,0:T(8,128)(2,1)} %get-tuple-element.22), channel_id=1, source_target_pairs={{0,480},{32,0},{64,32},{96,64},{128,96},{160,128},{192,160},{224,1... | collective-permute-start | bytes 442376 | tf_op jit(solution)/shard_map/ppermute | solution.py:652
  25.0 1.0 %shard_map.231 = bf16[16,32,128]{2,1,0:T(8,128)(2,1)} custom-call(bf16[4,2,32,256]{3,2,1,0:T(8,128)(2,1)S(1)} %copy-done.4, f32[32,8,128]{2,1,0:T(8,128)S(1)} %all-to-all-done.refs_1_), custom_call_target="tpu_custom_call" | custom-call | flops 1100000000 | bytes 1000000 | tf_op jit(solution)/shard_map/pallas_call | solution.py:620
  25.9 0.0 copy-start.2
  25.9 0.0 copy-start.3
  26.0 13.2 %all-to-all-start.1 = ((bf16[16,32,128]{2,1,0:T(8,128)(2,1)}), bf16[16,32,128]{2,1,0:T(8,128)(2,1)S(1)}, u32[]{:S(2)}, u32[]{:S(2)}) async-start(bf16[16,32,128]{2,1,0:T(8,128)(2,1)} %shard_map.231), calls=%async_computation.1 | async-start | bytes 262144 | tf_op jit(solution)/shard_map/all_to_all | solution.py:685
  39.1 0.6 copy.25.refs_0_
  39.8 0.6 copy-done.5
  40.4 0.0 copy-done.6
  40.4 3.7 %shard_map.232 = (bf16[80,3072]{1,0:T(8,128)(2,1)}, bf16[80,3072]{1,0:T(8,128)(2,1)}, bf16[288,224]{1,0:T(8,128)(2,1)}, bf16[160,144]{1,0:T(8,128)(2,1)}, bf16[2...) custom-call(f32[2,3,3]{2,1,0:T(4,128)} %copy.25.refs_0_, bf16[160,208]{1,0:T(8,128)(2,1)} %constant.43.clone.refs_1_, ...), custom_call_target="tpu_custom_call" | custom-call | flops 11000000 | bytes 10000 | tf_op jit(solution)/shard_map/pallas_call | solution.py:620
  44.2 2.6 %collective-permute-start.2 = (bf16[80,3072]{1,0:T(8,128)(2,1)}, bf16[80,3072]{1,0:T(8,128)(2,1)S(1)}, u32[]{:S(2)}, u32[]{:S(2)}) collective-permute-start(bf16[80,3072]{1,0:T(8,128)(2,1)} %get-tuple-element.28), channel_id=1, source_target_pairs={{0,1},{1,2},{2,3},{3,4},{4,5},{5,6},{6,7},{7,8},{8,9},{9,10},{10,1... | collective-permute-start | bytes 1474568 | tf_op jit(solution)/shard_map/ppermute | solution.py:652
  46.8 4.3 %all-to-all-done.1.refs_4_ = bf16[16,32,128]{2,1,0:T(8,128)(2,1)S(1)} async-done(((bf16[16,32,128]{2,1,0:T(8,128)(2,1)}), bf16[16,32,128]{2,1,0:T(8,128)(2,1)S(1)}, u32[]{:S(2)}, u32[]{:S(2)}) %all-to-all-start.1) | async-done | bytes 131104 | tf_op jit(solution)/shard_map/all_to_all | solution.py:685
  51.1 0.8 %copy-done = f32[128,128]{1,0:T(8,128)S(1)} copy-done((f32[128,128]{1,0:T(8,128)S(1)}, f32[128,128]{1,0:T(8,128)}, u32[]{:S(2)}) %copy-start) | copy-done | bytes 65560
  52.0 0.8 copy-done.1
  52.7 1.5 %shard_map.233 = f32[16,2,8,128]{3,2,1,0:T(8,128)} custom-call(bf16[2,2,128,512]{3,2,1,0:T(8,128)(2,1)S(1)} %copy-done.2, bf16[2,2,32,128]{3,2,1,0:T(8,128)(2,1)S(1)} %copy-done.1, bf16[2,2,128,32]{3,2,1,0:T(8,128)(2,1)S(1)} %copy-done.3, f32[128,128]{1,0:T(8,128)S(1)} %copy-done, bf16[16,32,128]{2,1,0:T(8,128)(2,1)S(1)} %all-to-all-done.1.refs_4_), custom_call_target="tpu_custom_call" | custom-call | flops 1100000000 | bytes 1000000 | tf_op jit(solution)/shard_map/pallas_call | solution.py:620
  54.2 7.2 %all-to-all-start.2 = ((f32[32,8,128]{2,1,0:T(8,128)}), f32[32,8,128]{2,1,0:T(8,128)S(1)}, u32[]{:S(2)}, u32[]{:S(2)}) async-start(f32[32,8,128]{2,1,0:T(8,128)} %bitcast.3), calls=%async_computation.2 | async-start | bytes 262144 | tf_op jit(solution)/shard_map/all_to_all | solution.py:663
  61.5 0.8 copy-done.9
  62.3 0.2 copy-done.10
  62.5 8.8 %shard_map.234.refs_3_ = bf16[2,192,1024]{2,1,0:T(8,128)(2,1)} custom-call(bf16[288,224]{1,0:T(8,128)(2,1)} %get-tuple-element.23.refs_0_, bf16[144,144]{1,0:T(8,128)(2,1)} %constant.44.clone.refs_1_, bf16[160,3072]{1,0:T(8,128)(2,1)} %get-tuple-element.27.refs_2_, bf16[24,3072]{1,0:T(8,128)(2,1)} %copy-done.5, bf16[24,3072]{1,0:T(8,128)(2,1)} %copy-done.6, ...), custom_call_target="tpu_custom_call" | custom-call | flops 7699999744 | bytes 7000000 | tf_op jit(solution)/shard_map/pallas_call | solution.py:620
  71.3 0.6 copy-done.7
  71.9 4.4 %shard_map.235 = (bf16[192,1024]{1,0:T(8,128)(2,1)}, bf16[192,1024]{1,0:T(8,128)(2,1)}) custom-call(bf16[256,1024]{1,0:T(8,128)(2,1)} %constant.49.clone.refs_0_, bf16[256,1024]{1,0:T(8,128)(2,1)} %constant.50.clone.refs_1_, bf16[2,4,192,256]{3,2,1,0:T(8,128)(2,1)} %constant.51.clone.refs_2_, bf16[2,192,1024]{2,1,0:T(8,128)(2,1)} %shard_map.234.refs_3_, ...), custom_call_target="tpu_custom_call" | custom-call | flops 3300000000 | bytes 3000000 | tf_op jit(solution)/shard_map/pallas_call | solution.py:620
  (19 shorter events, 0.0 us)
Async XLA Ops:
  0.6 24.3 %copy-start.4 = (bf16[4,2,32,256]{3,2,1,0:T(8,128)(2,1)S(1)}, bf16[4,2,32,256]{3,2,1,0:T(8,128)(2,1)}, u32[]{:S(2)}) copy-start(bf16[4,2,32,256]{3,2,1,0:T(8,128)(2,1)} %constant.45.clone.refs_0_) | copy-start | bytes 393220
  5.8 19.2 %all-to-all-start = ((f32[32,8,128]{2,1,0:T(8,128)}), f32[32,8,128]{2,1,0:T(8,128)S(1)}, u32[]{:S(2)}, u32[]{:S(2)}) async-start(f32[32,8,128]{2,1,0:T(8,128)} %get-tuple-element.18), calls=%async_computation | async-start | bytes 262144 | tf_op jit(solution)/shard_map/all_to_all | solution.py:663
  16.2 23.5 %collective-permute-start = (bf16[24,3072]{1,0:T(8,128)(2,1)}, bf16[24,3072]{1,0:T(8,128)(2,1)S(1)}, u32[]{:S(2)}, u32[]{:S(2)}) collective-permute-start(bf16[24,3072]{1,0:T(8,128)(2,1)} %get-tuple-element.21), channel_id=1, source_target_pairs={{0,32},{32,64},{64,96},{96,128},{128,160},{160,192},{192,224},{224... | collective-permute-start | bytes 442376 | tf_op jit(solution)/shard_map/ppermute | solution.py:652
  19.5 19.6 %copy-start.8 = (f32[2,3,3]{2,0,1:T(2,128)S(1)}, f32[2,3,3]{2,0,1:T(2,128)}, u32[]{:S(2)}) copy-start(f32[2,3,3]{2,0,1:T(2,128)} %param.25) | copy-start | bytes 220
  19.5 20.2 %collective-permute-start.1 = (bf16[24,3072]{1,0:T(8,128)(2,1)}, bf16[24,3072]{1,0:T(8,128)(2,1)S(1)}, u32[]{:S(2)}, u32[]{:S(2)}) collective-permute-start(bf16[24,3072]{1,0:T(8,128)(2,1)} %get-tuple-element.22), channel_id=1, source_target_pairs={{0,480},{32,0},{64,32},{96,64},{128,96},{160,128},{192,160},{224,1... | collective-permute-start | bytes 442376 | tf_op jit(solution)/shard_map/ppermute | solution.py:652
  25.9 25.2 %copy-start.2 = (bf16[2,2,128,512]{3,2,1,0:T(8,128)(2,1)S(1)}, bf16[2,2,128,512]{3,2,1,0:T(8,128)(2,1)}, u32[]{:S(2)}) copy-start(bf16[2,2,128,512]{3,2,1,0:T(8,128)(2,1)} %constant.47.clone.refs_0_) | copy-start | bytes 1572868
  25.9 25.2 %copy-start.3 = (bf16[2,2,128,32]{3,2,1,0:T(8,128)(2,1)S(1)}, bf16[2,2,128,32]{3,2,1,0:T(8,128)(2,1)}, u32[]{:S(2)}) copy-start(bf16[2,2,128,32]{3,2,1,0:T(8,128)(2,1)} %constant.46.clone.refs_2_) | copy-start | bytes 98308
  26.0 25.2 %all-to-all-start.1 = ((bf16[16,32,128]{2,1,0:T(8,128)(2,1)}), bf16[16,32,128]{2,1,0:T(8,128)(2,1)S(1)}, u32[]{:S(2)}, u32[]{:S(2)}) async-start(bf16[16,32,128]{2,1,0:T(8,128)(2,1)} %shard_map.231), calls=%async_computation.1 | async-start | bytes 262144 | tf_op jit(solution)/shard_map/all_to_all | solution.py:685
  39.7 0.7 copy-start.5
  39.7 0.7 copy-start.6
  44.2 17.3 %collective-permute-start.2 = (bf16[80,3072]{1,0:T(8,128)(2,1)}, bf16[80,3072]{1,0:T(8,128)(2,1)S(1)}, u32[]{:S(2)}, u32[]{:S(2)}) collective-permute-start(bf16[80,3072]{1,0:T(8,128)(2,1)} %get-tuple-element.28), channel_id=1, source_target_pairs={{0,1},{1,2},{2,3},{3,4},{4,5},{5,6},{6,7},{7,8},{8,9},{9,10},{10,1... | collective-permute-start | bytes 1474568 | tf_op jit(solution)/shard_map/ppermute | solution.py:652
  46.8 14.7 %collective-permute-start.3 = (bf16[80,3072]{1,0:T(8,128)(2,1)}, bf16[80,3072]{1,0:T(8,128)(2,1)S(1)}, u32[]{:S(2)}, u32[]{:S(2)}) collective-permute-start(bf16[80,3072]{1,0:T(8,128)(2,1)} %get-tuple-element.29), channel_id=1, source_target_pairs={{0,31},{1,0},{2,1},{3,2},{4,3},{5,4},{6,5},{7,6},{8,7},{9,8},{10,9... | collective-permute-start | bytes 1474568 | tf_op jit(solution)/shard_map/ppermute | solution.py:652
  51.1 0.8 %copy-start = (f32[128,128]{1,0:T(8,128)S(1)}, f32[128,128]{1,0:T(8,128)}, u32[]{:S(2)}) copy-start(f32[128,128]{1,0:T(8,128)} %get-tuple-element.25.refs_3_) | copy-start | bytes 196612
  52.0 0.8 copy-start.1
  54.2 17.0 %all-to-all-start.2 = ((f32[32,8,128]{2,1,0:T(8,128)}), f32[32,8,128]{2,1,0:T(8,128)S(1)}, u32[]{:S(2)}, u32[]{:S(2)}) async-start(f32[32,8,128]{2,1,0:T(8,128)} %bitcast.3), calls=%async_computation.2 | async-start | bytes 262144 | tf_op jit(solution)/shard_map/all_to_all | solution.py:663
  61.5 0.8 %copy-start.9 = (bf16[80,3072]{1,0:T(8,128)(2,1)}, bf16[80,3072]{1,0:T(8,128)(2,1)S(1)}, u32[]{:S(2)}) copy-start(bf16[80,3072]{1,0:T(8,128)(2,1)S(1)} %collective-permute-done.2.refs_5_) | copy-start | bytes 1474564
  61.5 0.9 %copy-start.10 = (bf16[80,3072]{1,0:T(8,128)(2,1)}, bf16[80,3072]{1,0:T(8,128)(2,1)S(1)}, u32[]{:S(2)}) copy-start(bf16[80,3072]{1,0:T(8,128)(2,1)S(1)} %collective-permute-done.3.refs_6_) | copy-start | bytes 1474564
  71.2 0.7 copy-start.7

commit v3 on v2

--- a/solution.py
+++ b/solution.py
@@ -373,7 +373,7 @@
         out_ref[n] = out
 
 
-def ends_kernel(stencil_ref, send_ref, loc_ref, up_ref, down_ref, tap_ref, tap_back_ref, places_ref, gains_ref, left_ref, right_ref, lead_ref, lead_back_ref, my_places_ref, my_gains_ref):
+def ends_kernel(stencil_ref, send_ref, loc_ref, up_ref, down_ref, tap_ref, tap_back_ref, places_ref, gains_ref, left_ref, right_ref, lead_ref, lead_back_ref, my_ref):
     known = jnp.concatenate([loc_ref[...], stack([up_ref[...], down_ref[...]])], axis=0)
     moved = mm(send_ref[...], known).astype(BF)
     left_ref[...] = moved[: MSG_ROWS[2]]
@@ -383,7 +383,7 @@
     taps = [stencil_ref[n // 9, n // 3 % 3, n % 3] for n in range(18)]
     lead_ref[:QROWS], lead_ref[QROWS:] = split(tap_matrix(tap_ref[...], taps))
     lead_back_ref[:INNER], lead_back_ref[INNER:] = split(tap_matrix(tap_back_ref[...], taps))
-    my_places_ref[...] = places_ref[...]
+    my_ref[2 * MODES * MODES :] = places_ref[...]
     gains = gains_ref[...]
     own = (lax.axis_index("row") * 2 + lax.axis_index("col") % 2) % 4
     group = lax.broadcasted_iota(jnp.int32, gains.shape, 1) // SUB
@@ -392,19 +392,22 @@
         for t in range(2):
             moved = pltpu.roll(gains, (t - s) % 4 * SUB, 1) if s != t else gains
             total = jnp.where((group == t) & (own == s), moved, total)
-    my_gains_ref[...] = total
-
-
-def modes_kernel(scale, across_ref, table_ref, rows_ref, gains_ref, parts_ref, out_ref):
+    my_ref[: 2 * MODES * MODES] = total
+
+
+def modes_kernel(scale, across_ref, rows_ref, my_ref, parts_ref, out_ref):
     parts = parts_ref[...].reshape(-1, TILE)
     half = TILE // 2
     modes = mm(across_ref[0, 0], parts) + mm(across_ref[0, 1], parts)
     modes = modes + pltpu.roll(mm(across_ref[1, 0], parts) + mm(across_ref[1, 1], parts), half, 1)
-    coeffs = gains_ref[...] * modes * scale
+    count = modes.shape[0]
+    coeffs = split(my_ref[:count] * modes * scale)
     near = lax.broadcasted_iota(jnp.int32, (4 * MODES, TILE), 1) < half
-    wide = jnp.where(
-        near, mm3(table_ref.at[0], coeffs), pltpu.roll(mm3(table_ref.at[1], coeffs), half, 1)
-    )
+    wide = []
+    for core in range(2):
+        high, low = split(my_ref[count + core * 4 * MODES : count + (core + 1) * 4 * MODES])
+        wide.append(mm(high, coeffs[0]) + mm(high, coeffs[1]) + mm(low, coeffs[0]))
+    wide = jnp.where(near, wide[0], pltpu.roll(wide[1], half, 1))
     first, second = mm3(rows_ref.at[0], wide), mm3(rows_ref.at[1], wide)
     near = lax.broadcasted_iota(jnp.int32, first.shape, 1) < half
     shape = (out_ref.shape[0], 8, TILE)
@@ -425,7 +428,7 @@
     return total
 
 
-def detail_kernel(lead_ref, pick_ref, loc_ref, up_ref, down_ref, left_ref, right_ref, mix_ref, lead_back_ref, wh_ref, wl_ref, scatter_ref, out_ref, scratch):
+def detail_kernel(lead_ref, pick_ref, loc_ref, up_ref, down_ref, left_ref, right_ref, mix_ref, lead_back_ref, filter_ref, scatter_ref, out_ref, scratch):
     messages = [ref[...].astype(F32) for ref in (up_ref, down_ref, left_ref, right_ref)]
     details = [message[:cut] for message, cut in zip(messages, MSG_CUT)]
     others = [message[cut:] for message, cut in zip(messages, MSG_CUT)]
@@ -456,33 +459,32 @@
         grad = (back[band * QROWS : (band + 1) * QROWS] * derivatives[band]).astype(BF)
         found = mm(lead_back, grad)
         scratch[1, band] = (found[:INNER] + found[INNER:]).astype(BF)
-    found = synthesize(None, scratch, slice(G1, INNER), wh_ref, wl_ref)
-    found = synthesize([[part.astype(BF) for part in place(out)] for out in found], scratch, slice(0, G1), wh_ref, wl_ref)
+    found = synthesize(None, scratch, slice(G1, INNER), filter_ref)
+    found = synthesize([[part.astype(BF) for part in place(out)] for out in found], scratch, slice(0, G1), filter_ref)
     scatter = scatter_ref[...]
     for n in range(2):
         for k, block in enumerate(place(found[n])):
             out_ref[n, :, k * QW : (k + 1) * QW] = mm(scatter, block.astype(BF)).astype(BF)
 
 
-def finish_kernel(wh_ref, wl_ref, left_ref, part_ref, coarse_ref, up_ref, down_ref):
+def finish_kernel(filter_ref, left_ref, part_ref, coarse_ref, up_ref, down_ref):
     count = K * G2
     tiles = unpack_channels(coarse_ref)
     states = [
         [jnp.concatenate(own[2 * m : 2 * m + 2], axis=1) for m in range(K)] for own in tiles
     ]
-    wide = times_filter(jnp.concatenate(states[0] + states[1], axis=0), wh_ref[...], wl_ref[...])
+    wide = mm(jnp.concatenate(states[0] + states[1], axis=0).astype(BF), filter_ref[...]).astype(BF)
     for n, ref in enumerate((up_ref, down_ref)):
         rows = wide[n * count : (n + 1) * count]
-        high, low = split(jnp.concatenate([rows[:, j * QW : (j + 1) * QW] for j in range(4)], axis=0))
+        right = jnp.concatenate([rows[:, j * QW : (j + 1) * QW] for j in range(4)], axis=0)
         for k in range(K):
             lanes = slice(k * QW, (k + 1) * QW)
-            left_high, left_low = left_ref[0, k], left_ref[1, k]
-            found = mm(left_high, high) + mm(left_high, low) + mm(left_low, high)
+            found = mm(left_ref[k], right)
             ref[:, lanes] = (part_ref[n, :, lanes] + found).astype(BF)
         ref.send()
 
 
-def synthesize(states, scratch, rows, wh_ref, wl_ref):
+def synthesize(states, scratch, rows, filter_ref):
     lefts = []
     for n in range(2):
         for band in range(2):
@@ -494,7 +496,7 @@
                     pair = [jnp.zeros_like(detail) if states is None else states[n][m], detail]
                 lefts.append(jnp.concatenate(pair, axis=1))
     left = jnp.concatenate(lefts, axis=0)
-    wide = mm(left, wh_ref[...]) + mm(left, wl_ref[...])
+    wide = mm(left, filter_ref[...])
     count = rows.stop - rows.start
     out = []
     for n in range(2):
@@ -543,8 +545,9 @@
             places[:, :, 1, u, v, 1, u] = cosine[v]
     places = places.reshape(chip_count, 2, 2 * MODES * MODES, 2 * MODES * W2)
     across = places.transpose(1, 2, 0, 3).reshape(2, 2 * MODES * MODES, -1)
-    places = places.transpose(0, 1, 3, 2)
-    return [jnp.asarray(np.stack(halves(part), axis=part.ndim - 2)) for part in (along, back, across, places)]
+    places = places.transpose(0, 1, 3, 2).reshape(chip_count, 4 * MODES * W2, -1)
+    found = [jnp.asarray(np.stack(halves(part), axis=part.ndim - 2)) for part in (along, back, across)]
+    return found + [jnp.asarray(places.astype(np.float32))]
 
 
 class Fetched:
@@ -634,7 +637,7 @@
 def body(field, mix, stencil, spectral, cotangent):
     row_count, col_count = lax.axis_size("row"), lax.axis_size("col")
     wh, wl = [jnp.asarray(part) for part in halves(COL_FILTER)]
-    wht, wlt = [jnp.asarray(np.ascontiguousarray(part.T)) for part in halves(COL_FILTER)]
+    wht = jnp.asarray(np.ascontiguousarray(halves(COL_FILTER)[0].T))
     gather, scatter, send_side, send_ends, pick = [
         jnp.asarray(np.ascontiguousarray(part).astype(ml_dtypes.bfloat16))
         for part in (gather_table(), gather_table().T, SEND_SIDE, SEND_ENDS, PICK_BACK)
@@ -651,8 +654,8 @@
         count = lax.axis_size(axis)
         return lax.ppermute(message, axis, [(n, (n - step) % count) for n in range(count)])
 
-    coarse_back = [table(part.T) for part in halves(COARSE_RIGHT)]
-    left_back = table(np.stack([part.transpose(0, 2, 1) for part in halves(COARSE_LEFT)]))
+    coarse_back = table(halves(COARSE_RIGHT)[0].T)
+    left_back = table(halves(COARSE_LEFT)[0].transpose(0, 2, 1))
     plane = [
         [r * col_count + 2 * z + core for r in range(row_count) for core in range(2)]
         for z in range(chip_count)
@@ -683,11 +686,11 @@
     )
     part, loc = lax.optimization_barrier((part, loc))
     part = lax.all_to_all(part, "col", 0, 0, tiled=True, axis_index_groups=chips)
-    to_left, to_right, lead, lead_back, my_places, my_gains = call(
+    to_left, to_right, lead, lead_back, mine = call(
         ends_kernel,
         [shape((count, 3 * F), BF) for count in MSG_ROWS[2:]]
         + [shape((2 * QROWS, STACK_ROWS[0]), BF), shape((2 * INNER, QROWS), BF)]
-        + [shape(places.shape[1:], BF), shape((2 * MODES * MODES, TILE), F32)],
+        + [shape((2 * MODES * MODES + places.shape[1], TILE), F32)],
         (stencil, send_ends, loc, up, down, jnp.asarray(TAP_AT), jnp.asarray(TAP_BACK), places,
          spectral.reshape(-1, F)),
         0.01,
@@ -704,9 +707,9 @@
     part = call(
         functools.partial(modes_kernel, 1.0 / math.sqrt(row_count * H2 * col_count * W2)),
         shape((row_count, 2, 8, TILE), F32),
-        (across, my_places, back, my_gains, part),
+        (across, back, mine, part),
         1,
-        near=5,
+        near=4,
         near_out=True,
         limit=8,
     )
@@ -715,14 +718,14 @@
     details = call(
         detail_kernel,
         shape((2, FI * FJ, F), BF),
-        (lead, pick, loc, up, down, left, right, mix, lead_back, wht, wlt, scatter),
+        (lead, pick, loc, up, down, left, right, mix, lead_back, wht, scatter),
         7,
         scratch=[pltpu.VMEM((2, 3, INNER, F), BF)],
     )
     layer_out, grad_field = call(
         finish_kernel,
         [shape((FI * FJ, F), BF)] * 2,
-        (*coarse_back, left_back, details, part),
+        (coarse_back, left_back, details, part),
         3,
         near=1,
     )

time: 76.9 us -> 74.7 us (0.971)
  Pallas kernels: 24.5 us -> 23 us
    pallas_call x6, Pallas kernels: 24.5 us -> 23 us  [call(): pl.pallas_call(wrapped, out_shape=outs, in_specs=[pl.BlockSpec(memory_spa...]
    unnamed x23 -> x21, local copies, waits for them, and re-layouts: 4.49 us -> 3.78 us
  transfers between devices with their start and end apart: 7 -> 7, of which waited for: 1 -> 1; matrix products, arithmetic and copies ran while one was open for 1% -> 1% of each run, Pallas kernels for 20% -> 19%
where the time goes in v3:
time: 74.7 us; the launch traced here: 74.2 us
  starting transfers between devices  42.1 us (56%)
  Pallas kernels  23 us (31%)
  waiting for transfers between devices  4.39 us (6%)
  local copies, waits for them, and re-layouts  3.78 us (5%)
  between operations  0.83 us (1%)
    pallas_call x6, Pallas kernels, call(): pl.pallas_call(wrapped, out_shape=outs, in_specs=[pl.BlockSpec(memory_spa...  23 us
    all_to_all x2, starting transfers between devices, over_plane(): lax.all_to_all(pieces, ('row', 'col'), 0, 0, tiled=True, axis_index_group...  17.7 us
    all_to_all x1, starting transfers between devices, body(): lax.all_to_all(part, 'col', 0, 0, tiled=True, axis_index_groups=chips)  13.1 us
    ppermute x4, starting transfers between devices, shift(): lax.ppermute(message, axis, [(n, (n - step) % count) for n in range(count)])  11.3 us
    all_to_all x1, waiting for transfers between devices, body(): lax.all_to_all(part, 'col', 0, 0, tiled=True, axis_index_groups=chips)  4.37 us
    unnamed x21, local copies, waits for them, and re-layouts  3.78 us
  transfers between devices with their start and end apart: 7, of which 1 were waited for; matrix products, arithmetic and copies ran while one was open for 1% of the time, Pallas kernels for 19%

profile of v3, /device:TPU:1, one launch (start us, length us, event | category | flops | bytes accessed | tf_op | source)
XLA Modules:
  0.0 74.2 jit_solution(15129942071317055700)
XLA Ops:
  0.6 0.0 copy-start.3
  0.6 5.1 %shard_map.212 = (bf16[160,3072]{1,0:T(8,128)(2,1)}, bf16[24,3072]{1,0:T(8,128)(2,1)}, bf16[24,3072]{1,0:T(8,128)(2,1)}, f32[32,8,128]{2,1,0:T(8,128)}) custom-call(bf16[192,1024]{1,0:T(8,128)(2,1)} %bitcast.7, bf16[192,1024]{1,0:T(8,128)(2,1)} %bitcast.8, bf16[256,192]{1,0:T(8,128)(2,1)} %constant.35.clone.refs_2_, ...), custom_call_target="tpu_custom_call" | custom-call | flops 4400000000 | bytes 4000000 | tf_op jit(solution)/shard_map/pallas_call | solution.py:623
  5.8 10.4 %all-to-all-start = ((f32[32,8,128]{2,1,0:T(8,128)}), f32[32,8,128]{2,1,0:T(8,128)S(1)}, u32[]{:S(2)}, u32[]{:S(2)}) async-start(f32[32,8,128]{2,1,0:T(8,128)} %get-tuple-element.17), calls=%async_computation | async-start | bytes 262144 | tf_op jit(solution)/shard_map/all_to_all | solution.py:666
  16.2 3.3 %collective-permute-start = (bf16[24,3072]{1,0:T(8,128)(2,1)}, bf16[24,3072]{1,0:T(8,128)(2,1)S(1)}, u32[]{:S(2)}, u32[]{:S(2)}) collective-permute-start(bf16[24,3072]{1,0:T(8,128)(2,1)} %get-tuple-element.20), channel_id=1, source_target_pairs={{0,32},{32,64},{64,96},{96,128},{128,160},{160,192},{192,224},{224... | collective-permute-start | bytes 442376 | tf_op jit(solution)/shard_map/ppermute | solution.py:655
  19.5 0.0 copy-start.7
  19.5 5.4 %collective-permute-start.1 = (bf16[24,3072]{1,0:T(8,128)(2,1)}, bf16[24,3072]{1,0:T(8,128)(2,1)S(1)}, u32[]{:S(2)}, u32[]{:S(2)}) collective-permute-start(bf16[24,3072]{1,0:T(8,128)(2,1)} %get-tuple-element.21), channel_id=1, source_target_pairs={{0,480},{32,0},{64,32},{96,64},{128,96},{160,128},{192,160},{224,1... | collective-permute-start | bytes 442376 | tf_op jit(solution)/shard_map/ppermute | solution.py:655
  25.0 1.0 %shard_map.213 = bf16[16,32,128]{2,1,0:T(8,128)(2,1)} custom-call(bf16[4,2,32,256]{3,2,1,0:T(8,128)(2,1)S(1)} %copy-done.3, f32[32,8,128]{2,1,0:T(8,128)S(1)} %all-to-all-done.refs_1_), custom_call_target="tpu_custom_call" | custom-call | flops 1100000000 | bytes 1000000 | tf_op jit(solution)/shard_map/pallas_call | solution.py:623
  25.9 0.0 copy-start.1
  26.0 0.0 copy-start.2
  26.0 13.1 %all-to-all-start.1 = ((bf16[16,32,128]{2,1,0:T(8,128)(2,1)}), bf16[16,32,128]{2,1,0:T(8,128)(2,1)S(1)}, u32[]{:S(2)}, u32[]{:S(2)}) async-start(bf16[16,32,128]{2,1,0:T(8,128)(2,1)} %shard_map.213), calls=%async_computation.1 | async-start | bytes 262144 | tf_op jit(solution)/shard_map/all_to_all | solution.py:688
  39.1 0.6 copy.23.refs_0_
  39.7 0.6 copy-done.4
  40.4 0.0 copy-done.5
  40.4 3.7 %shard_map.214 = (bf16[80,3072]{1,0:T(8,128)(2,1)}, bf16[80,3072]{1,0:T(8,128)(2,1)}, bf16[288,224]{1,0:T(8,128)(2,1)}, bf16[160,144]{1,0:T(8,128)(2,1)}, f32[192,128]{1,0:T(8,128)}) custom-call(f32[2,3,3]{2,1,0:T(4,128)} %copy.23.refs_0_, bf16[160,208]{1,0:T(8,128)(2,1)} %constant.38.clone.refs_1_, bf16[160,3072]{1,0:T(8,128)(2,1)} %get-tuple-element.25.refs_2_, ...), custom_call_target="tpu_custom_call" | custom-call | flops 11000000 | bytes 10000 | tf_op jit(solution)/shard_map/pallas_call | solution.py:623
  44.1 2.6 %collective-permute-start.2 = (bf16[80,3072]{1,0:T(8,128)(2,1)}, bf16[80,3072]{1,0:T(8,128)(2,1)S(1)}, u32[]{:S(2)}, u32[]{:S(2)}) collective-permute-start(bf16[80,3072]{1,0:T(8,128)(2,1)} %get-tuple-element.26), channel_id=1, source_target_pairs={{0,1},{1,2},{2,3},{3,4},{4,5},{5,6},{6,7},{7,8},{8,9},{9,10},{10,1... | collective-permute-start | bytes 1474568 | tf_op jit(solution)/shard_map/ppermute | solution.py:655
  46.7 4.4 %all-to-all-done.1.refs_3_ = bf16[16,32,128]{2,1,0:T(8,128)(2,1)S(1)} async-done(((bf16[16,32,128]{2,1,0:T(8,128)(2,1)}), bf16[16,32,128]{2,1,0:T(8,128)(2,1)S(1)}, u32[]{:S(2)}, u32[]{:S(2)}) %all-to-all-start.1) | async-done | bytes 131104 | tf_op jit(solution)/shard_map/all_to_all | solution.py:688
  51.1 0.9 %copy-done = f32[192,128]{1,0:T(8,128)S(1)} copy-done((f32[192,128]{1,0:T(8,128)S(1)}, f32[192,128]{1,0:T(8,128)}, u32[]{:S(2)}) %copy-start) | copy-done | bytes 98328
  52.0 1.5 %shard_map.215 = f32[16,2,8,128]{3,2,1,0:T(8,128)} custom-call(bf16[2,2,128,512]{3,2,1,0:T(8,128)(2,1)S(1)} %copy-done.1, bf16[2,2,128,32]{3,2,1,0:T(8,128)(2,1)S(1)} %copy-done.2, f32[192,128]{1,0:T(8,128)S(1)} %copy-done, bf16[16,32,128]{2,1,0:T(8,128)(2,1)S(1)} %all-to-all-done.1.refs_3_), custom_call_target="tpu_custom_call" | custom-call | flops 1100000000 | bytes 1000000 | tf_op jit(solution)/shard_map/pallas_call | solution.py:623
  53.5 7.2 %all-to-all-start.2 = ((f32[32,8,128]{2,1,0:T(8,128)}), f32[32,8,128]{2,1,0:T(8,128)S(1)}, u32[]{:S(2)}, u32[]{:S(2)}) async-start(f32[32,8,128]{2,1,0:T(8,128)} %bitcast.3), calls=%async_computation.2 | async-start | bytes 262144 | tf_op jit(solution)/shard_map/all_to_all | solution.py:666
  60.8 0.8 %copy-done.8 = bf16[80,3072]{1,0:T(8,128)(2,1)} copy-done((bf16[80,3072]{1,0:T(8,128)(2,1)}, bf16[80,3072]{1,0:T(8,128)(2,1)S(1)}, u32[]{:S(2)}) %copy-start.8) | copy-done | bytes 491544
  61.6 0.2 copy-done.9
  61.8 8.1 %shard_map.216.refs_2_ = bf16[2,192,1024]{2,1,0:T(8,128)(2,1)} custom-call(bf16[288,224]{1,0:T(8,128)(2,1)} %get-tuple-element.22.refs_0_, bf16[144,144]{1,0:T(8,128)(2,1)} %constant.39.clone.refs_1_, bf16[160,3072]{1,0:T(8,128)(2,1)} %get-tuple-element.25.refs_2_, bf16[24,3072]{1,0:T(8,128)(2,1)} %copy-done.4, bf16[24,3072]{1,0:T(8,128)(2,1)} %copy-done.5, ...), custom_call_target="tpu_custom_call" | custom-call | flops 7699999744 | bytes 7000000 | tf_op jit(solution)/shard_map/pallas_call | solution.py:623
  69.9 0.6 copy-done.6
  70.5 3.6 %shard_map.217 = (bf16[192,1024]{1,0:T(8,128)(2,1)}, bf16[192,1024]{1,0:T(8,128)(2,1)}) custom-call(bf16[256,1024]{1,0:T(8,128)(2,1)} %constant.44.clone.refs_0_, bf16[4,192,256]{2,1,0:T(8,128)(2,1)} %constant.45.clone.refs_1_, bf16[2,192,1024]{2,1,0:T(8,128)(2,1)} %shard_map.216.refs_2_, f32[32,8,128]{2,1,0:T(8,128)} %copy-done.6), custom_call_target="tpu_custom_call" | custom-call | flops 3300000000 | bytes 3000000 | tf_op jit(solution)/shard_map/pallas_call | solution.py:623
  (17 shorter events, 0.0 us)
Async XLA Ops:
  0.6 24.3 %copy-start.3 = (bf16[4,2,32,256]{3,2,1,0:T(8,128)(2,1)S(1)}, bf16[4,2,32,256]{3,2,1,0:T(8,128)(2,1)}, u32[]{:S(2)}) copy-start(bf16[4,2,32,256]{3,2,1,0:T(8,128)(2,1)} %constant.40.clone.refs_0_) | copy-start | bytes 393220
  5.8 19.2 %all-to-all-start = ((f32[32,8,128]{2,1,0:T(8,128)}), f32[32,8,128]{2,1,0:T(8,128)S(1)}, u32[]{:S(2)}, u32[]{:S(2)}) async-start(f32[32,8,128]{2,1,0:T(8,128)} %get-tuple-element.17), calls=%async_computation | async-start | bytes 262144 | tf_op jit(solution)/shard_map/all_to_all | solution.py:666
  16.2 23.5 %collective-permute-start = (bf16[24,3072]{1,0:T(8,128)(2,1)}, bf16[24,3072]{1,0:T(8,128)(2,1)S(1)}, u32[]{:S(2)}, u32[]{:S(2)}) collective-permute-start(bf16[24,3072]{1,0:T(8,128)(2,1)} %get-tuple-element.20), channel_id=1, source_target_pairs={{0,32},{32,64},{64,96},{96,128},{128,160},{160,192},{192,224},{224... | collective-permute-start | bytes 442376 | tf_op jit(solution)/shard_map/ppermute | solution.py:655
  19.5 19.6 %copy-start.7 = (f32[2,3,3]{2,0,1:T(2,128)S(1)}, f32[2,3,3]{2,0,1:T(2,128)}, u32[]{:S(2)}) copy-start(f32[2,3,3]{2,0,1:T(2,128)} %param.23) | copy-start | bytes 220
  19.5 20.2 %collective-permute-start.1 = (bf16[24,3072]{1,0:T(8,128)(2,1)}, bf16[24,3072]{1,0:T(8,128)(2,1)S(1)}, u32[]{:S(2)}, u32[]{:S(2)}) collective-permute-start(bf16[24,3072]{1,0:T(8,128)(2,1)} %get-tuple-element.21), channel_id=1, source_target_pairs={{0,480},{32,0},{64,32},{96,64},{128,96},{160,128},{192,160},{224,1... | collective-permute-start | bytes 442376 | tf_op jit(solution)/shard_map/ppermute | solution.py:655
  25.9 25.2 %copy-start.1 = (bf16[2,2,128,512]{3,2,1,0:T(8,128)(2,1)S(1)}, bf16[2,2,128,512]{3,2,1,0:T(8,128)(2,1)}, u32[]{:S(2)}) copy-start(bf16[2,2,128,512]{3,2,1,0:T(8,128)(2,1)} %constant.42.clone.refs_0_) | copy-start | bytes 1572868
  26.0 25.2 %copy-start.2 = (bf16[2,2,128,32]{3,2,1,0:T(8,128)(2,1)S(1)}, bf16[2,2,128,32]{3,2,1,0:T(8,128)(2,1)}, u32[]{:S(2)}) copy-start(bf16[2,2,128,32]{3,2,1,0:T(8,128)(2,1)} %constant.41.clone.refs_1_) | copy-start | bytes 98308
  26.0 25.1 %all-to-all-start.1 = ((bf16[16,32,128]{2,1,0:T(8,128)(2,1)}), bf16[16,32,128]{2,1,0:T(8,128)(2,1)S(1)}, u32[]{:S(2)}, u32[]{:S(2)}) async-start(bf16[16,32,128]{2,1,0:T(8,128)(2,1)} %shard_map.213), calls=%async_computation.1 | async-start | bytes 262144 | tf_op jit(solution)/shard_map/all_to_all | solution.py:688
  39.7 0.7 copy-start.4
  39.7 0.7 copy-start.5
  44.1 16.6 %collective-permute-start.2 = (bf16[80,3072]{1,0:T(8,128)(2,1)}, bf16[80,3072]{1,0:T(8,128)(2,1)S(1)}, u32[]{:S(2)}, u32[]{:S(2)}) collective-permute-start(bf16[80,3072]{1,0:T(8,128)(2,1)} %get-tuple-element.26), channel_id=1, source_target_pairs={{0,1},{1,2},{2,3},{3,4},{4,5},{5,6},{6,7},{7,8},{8,9},{9,10},{10,1... | collective-permute-start | bytes 1474568 | tf_op jit(solution)/shard_map/ppermute | solution.py:655
  46.7 14.1 %collective-permute-start.3 = (bf16[80,3072]{1,0:T(8,128)(2,1)}, bf16[80,3072]{1,0:T(8,128)(2,1)S(1)}, u32[]{:S(2)}, u32[]{:S(2)}) collective-permute-start(bf16[80,3072]{1,0:T(8,128)(2,1)} %get-tuple-element.27), channel_id=1, source_target_pairs={{0,31},{1,0},{2,1},{3,2},{4,3},{5,4},{6,5},{7,6},{8,7},{9,8},{10,9... | collective-permute-start | bytes 1474568 | tf_op jit(solution)/shard_map/ppermute | solution.py:655
  51.1 0.9 %copy-start = (f32[192,128]{1,0:T(8,128)S(1)}, f32[192,128]{1,0:T(8,128)}, u32[]{:S(2)}) copy-start(f32[192,128]{1,0:T(8,128)} %get-tuple-element.23.refs_2_) | copy-start | bytes 294916
  53.5 16.4 %all-to-all-start.2 = ((f32[32,8,128]{2,1,0:T(8,128)}), f32[32,8,128]{2,1,0:T(8,128)S(1)}, u32[]{:S(2)}, u32[]{:S(2)}) async-start(f32[32,8,128]{2,1,0:T(8,128)} %bitcast.3), calls=%async_computation.2 | async-start | bytes 262144 | tf_op jit(solution)/shard_map/all_to_all | solution.py:666
  60.8 0.8 %copy-start.8 = (bf16[80,3072]{1,0:T(8,128)(2,1)}, bf16[80,3072]{1,0:T(8,128)(2,1)S(1)}, u32[]{:S(2)}) copy-start(bf16[80,3072]{1,0:T(8,128)(2,1)S(1)} %collective-permute-done.2.refs_5_) | copy-start | bytes 1474564
  60.8 0.9 %copy-start.9 = (bf16[80,3072]{1,0:T(8,128)(2,1)}, bf16[80,3072]{1,0:T(8,128)(2,1)S(1)}, u32[]{:S(2)}) copy-start(bf16[80,3072]{1,0:T(8,128)(2,1)S(1)} %collective-permute-done.3.refs_6_) | copy-start | bytes 1474564
  69.9 0.7 copy-start.6

commit v4 on v3

--- a/solution.py
+++ b/solution.py
@@ -350,8 +350,14 @@
     part_ref.send()
     loc_ref.send()
     moved = mm(send_ref[...], loc_ref[...])
-    up_ref[...] = moved[: MSG_ROWS[0]].astype(BF)
-    down_ref[...] = moved[MSG_ROWS[0] :].astype(BF)
+    first, second = by_parity(moved[: MSG_ROWS[0]], moved[MSG_ROWS[0] :])
+    up_ref[...] = first.astype(BF)
+    down_ref[...] = second.astype(BF)
+
+
+def by_parity(first, second):
+    even = lax.axis_index("row") % 2 == 0
+    return jnp.where(even, first, second), jnp.where(even, second, first)
 
 
 def stack(parts):
@@ -374,7 +380,8 @@
 
 
 def ends_kernel(stencil_ref, send_ref, loc_ref, up_ref, down_ref, tap_ref, tap_back_ref, places_ref, gains_ref, left_ref, right_ref, lead_ref, lead_back_ref, my_ref):
-    known = jnp.concatenate([loc_ref[...], stack([up_ref[...], down_ref[...]])], axis=0)
+    down, up = by_parity(up_ref[...].astype(F32), down_ref[...].astype(F32))
+    known = jnp.concatenate([loc_ref[...], stack([up, down])], axis=0)
     moved = mm(send_ref[...], known).astype(BF)
     left_ref[...] = moved[: MSG_ROWS[2]]
     left_ref.send()
@@ -430,6 +437,7 @@
 
 def detail_kernel(lead_ref, pick_ref, loc_ref, up_ref, down_ref, left_ref, right_ref, mix_ref, lead_back_ref, filter_ref, scatter_ref, out_ref, scratch):
     messages = [ref[...].astype(F32) for ref in (up_ref, down_ref, left_ref, right_ref)]
+    messages[:2] = by_parity(*messages[:2])[::-1]
     details = [message[:cut] for message, cut in zip(messages, MSG_CUT)]
     others = [message[cut:] for message, cut in zip(messages, MSG_CUT)]
     details = jnp.concatenate([loc_ref[:INNER], stack(details)], axis=0)
@@ -674,7 +682,10 @@
         4,
     )
     part = over_plane(part)
-    up, down = shift(to_up, *SIDES[0]), shift(to_down, *SIDES[1])
+    pairs = [(n, n ^ 1) for n in range(row_count)]
+    up = lax.ppermute(to_up, "row", pairs)
+    pairs = [(n, (n + 1 if n % 2 else n - 1) % row_count) for n in range(row_count)]
+    down = lax.ppermute(to_down, "row", pairs)
     part = call(
         along_kernel,
         shape((chip_count, 4 * MODES, TILE), BF),

time: 74.7 us -> 75.2 us (level)
    ppermute x0 -> x2, starting transfers between devices: none -> 9.28 us  [the longest x1 5.98 us: body(): down = lax.ppermute(to_down, 'row', pairs)]
    ppermute x4 -> x2, starting transfers between devices: 11.3 us -> 2.74 us  [shift(): lax.ppermute(message, axis, [(n, (n - step) % count) for n in range(count)])]
where the time goes in v4:
time: 75.2 us; the launch traced here: 74.7 us
  starting transfers between devices  42.7 us (57%)
  Pallas kernels  23.1 us (31%)
  waiting for transfers between devices  4.27 us (6%)
  local copies, waits for them, and re-layouts  3.78 us (5%)
  between operations  0.83 us (1%)
    pallas_call x6, Pallas kernels, call(): pl.pallas_call(wrapped, out_shape=outs, in_specs=[pl.BlockSpec(memory_spa...  23.1 us
    all_to_all x2, starting transfers between devices, over_plane(): lax.all_to_all(pieces, ('row', 'col'), 0, 0, tiled=True, axis_index_group...  17.5 us
    all_to_all x1, starting transfers between devices, body(): lax.all_to_all(part, 'col', 0, 0, tiled=True, axis_index_groups=chips)  13.2 us
    ppermute x1, starting transfers between devices, body(): down = lax.ppermute(to_down, 'row', pairs)  5.98 us
    all_to_all x1, waiting for transfers between devices, body(): lax.all_to_all(part, 'col', 0, 0, tiled=True, axis_index_groups=chips)  4.25 us
    unnamed x21, local copies, waits for them, and re-layouts  3.78 us
    ppermute x1, starting transfers between devices, body(): up = lax.ppermute(to_up, 'row', pairs)  3.3 us
    ppermute x2, starting transfers between devices, shift(): lax.ppermute(message, axis, [(n, (n - step) % count) for n in range(count)])  2.74 us
  transfers between devices with their start and end apart: 7, of which 1 were waited for; matrix products, arithmetic and copies ran while one was open for 1% of the time, Pallas kernels for 19%

profile of v4, /device:TPU:1, one launch (start us, length us, event | category | flops | bytes accessed | tf_op | source)
XLA Modules:
  0.0 74.7 jit_solution(14619427016413248225)
XLA Ops:
  0.6 0.0 copy-start.3
  0.6 5.1 %shard_map.212 = (bf16[160,3072]{1,0:T(8,128)(2,1)}, bf16[24,3072]{1,0:T(8,128)(2,1)}, bf16[24,3072]{1,0:T(8,128)(2,1)}, f32[32,8,128]{2,1,0:T(8,128)}) custom-call(bf16[192,1024]{1,0:T(8,128)(2,1)} %bitcast.7, bf16[192,1024]{1,0:T(8,128)(2,1)} %bitcast.8, bf16[256,192]{1,0:T(8,128)(2,1)} %constant.35.clone.refs_2_, ...), custom_call_target="tpu_custom_call" | custom-call | flops 4400000000 | bytes 4000000 | tf_op jit(solution)/shard_map/pallas_call | solution.py:631
  5.8 10.4 %all-to-all-start = ((f32[32,8,128]{2,1,0:T(8,128)}), f32[32,8,128]{2,1,0:T(8,128)S(1)}, u32[]{:S(2)}, u32[]{:S(2)}) async-start(f32[32,8,128]{2,1,0:T(8,128)} %get-tuple-element.17), calls=%async_computation | async-start | bytes 262144 | tf_op jit(solution)/shard_map/all_to_all | solution.py:674
  16.2 3.3 %collective-permute-start = (bf16[24,3072]{1,0:T(8,128)(2,1)}, bf16[24,3072]{1,0:T(8,128)(2,1)S(1)}, u32[]{:S(2)}, u32[]{:S(2)}) collective-permute-start(bf16[24,3072]{1,0:T(8,128)(2,1)} %get-tuple-element.20), channel_id=1, source_target_pairs={{0,32},{32,0},{64,96},{96,64},{128,160},{160,128},{192,224},{224,1... | collective-permute-start | bytes 442376 | tf_op jit(solution)/shard_map/ppermute | solution.py:686
  19.5 0.0 copy-start.7
  19.5 6.0 %collective-permute-start.1 = (bf16[24,3072]{1,0:T(8,128)(2,1)}, bf16[24,3072]{1,0:T(8,128)(2,1)S(1)}, u32[]{:S(2)}, u32[]{:S(2)}) collective-permute-start(bf16[24,3072]{1,0:T(8,128)(2,1)} %get-tuple-element.21), channel_id=1, source_target_pairs={{0,480},{32,64},{64,32},{96,128},{128,96},{160,192},{192,160},{224... | collective-permute-start | bytes 442376 | tf_op jit(solution)/shard_map/ppermute | solution.py:688
  25.5 1.0 %shard_map.213 = bf16[16,32,128]{2,1,0:T(8,128)(2,1)} custom-call(bf16[4,2,32,256]{3,2,1,0:T(8,128)(2,1)S(1)} %copy-done.3, f32[32,8,128]{2,1,0:T(8,128)S(1)} %all-to-all-done.refs_1_), custom_call_target="tpu_custom_call" | custom-call | flops 1100000000 | bytes 1000000 | tf_op jit(solution)/shard_map/pallas_call | solution.py:631
  26.5 0.0 copy-start.1
  26.5 0.0 copy-start.2
  26.5 13.2 %all-to-all-start.1 = ((bf16[16,32,128]{2,1,0:T(8,128)(2,1)}), bf16[16,32,128]{2,1,0:T(8,128)(2,1)S(1)}, u32[]{:S(2)}, u32[]{:S(2)}) async-start(bf16[16,32,128]{2,1,0:T(8,128)(2,1)} %shard_map.213), calls=%async_computation.1 | async-start | bytes 262144 | tf_op jit(solution)/shard_map/all_to_all | solution.py:699
  39.7 0.6 copy.23.refs_0_
  40.3 0.6 copy-done.4
  40.9 0.0 copy-done.5
  41.0 3.8 %shard_map.214 = (bf16[80,3072]{1,0:T(8,128)(2,1)}, bf16[80,3072]{1,0:T(8,128)(2,1)}, bf16[288,224]{1,0:T(8,128)(2,1)}, bf16[160,144]{1,0:T(8,128)(2,1)}, f32[192,128]{1,0:T(8,128)}) custom-call(f32[2,3,3]{2,1,0:T(4,128)} %copy.23.refs_0_, bf16[160,208]{1,0:T(8,128)(2,1)} %constant.38.clone.refs_1_, bf16[160,3072]{1,0:T(8,128)(2,1)} %get-tuple-element.25.refs_2_, ...), custom_call_target="tpu_custom_call" | custom-call | flops 11000000 | bytes 10000 | tf_op jit(solution)/shard_map/pallas_call | solution.py:631
  44.8 2.7 %collective-permute-start.2 = (bf16[80,3072]{1,0:T(8,128)(2,1)}, bf16[80,3072]{1,0:T(8,128)(2,1)S(1)}, u32[]{:S(2)}, u32[]{:S(2)}) collective-permute-start(bf16[80,3072]{1,0:T(8,128)(2,1)} %get-tuple-element.26), channel_id=1, source_target_pairs={{0,1},{1,2},{2,3},{3,4},{4,5},{5,6},{6,7},{7,8},{8,9},{9,10},{10,1... | collective-permute-start | bytes 1474568 | tf_op jit(solution)/shard_map/ppermute | solution.py:663
  47.5 4.3 %all-to-all-done.1.refs_3_ = bf16[16,32,128]{2,1,0:T(8,128)(2,1)S(1)} async-done(((bf16[16,32,128]{2,1,0:T(8,128)(2,1)}), bf16[16,32,128]{2,1,0:T(8,128)(2,1)S(1)}, u32[]{:S(2)}, u32[]{:S(2)}) %all-to-all-start.1) | async-done | bytes 131104 | tf_op jit(solution)/shard_map/all_to_all | solution.py:699
  51.8 0.9 %copy-done = f32[192,128]{1,0:T(8,128)S(1)} copy-done((f32[192,128]{1,0:T(8,128)S(1)}, f32[192,128]{1,0:T(8,128)}, u32[]{:S(2)}) %copy-start) | copy-done | bytes 98328
  52.7 1.5 %shard_map.215 = f32[16,2,8,128]{3,2,1,0:T(8,128)} custom-call(bf16[2,2,128,512]{3,2,1,0:T(8,128)(2,1)S(1)} %copy-done.1, bf16[2,2,128,32]{3,2,1,0:T(8,128)(2,1)S(1)} %copy-done.2, f32[192,128]{1,0:T(8,128)S(1)} %copy-done, bf16[16,32,128]{2,1,0:T(8,128)(2,1)S(1)} %all-to-all-done.1.refs_3_), custom_call_target="tpu_custom_call" | custom-call | flops 1100000000 | bytes 1000000 | tf_op jit(solution)/shard_map/pallas_call | solution.py:631
  54.2 7.1 %all-to-all-start.2 = ((f32[32,8,128]{2,1,0:T(8,128)}), f32[32,8,128]{2,1,0:T(8,128)S(1)}, u32[]{:S(2)}, u32[]{:S(2)}) async-start(f32[32,8,128]{2,1,0:T(8,128)} %bitcast.3), calls=%async_computation.2 | async-start | bytes 262144 | tf_op jit(solution)/shard_map/all_to_all | solution.py:674
  61.3 0.8 %copy-done.8 = bf16[80,3072]{1,0:T(8,128)(2,1)} copy-done((bf16[80,3072]{1,0:T(8,128)(2,1)}, bf16[80,3072]{1,0:T(8,128)(2,1)S(1)}, u32[]{:S(2)}) %copy-start.8) | copy-done | bytes 491544
  62.1 0.2 copy-done.9
  62.2 8.1 %shard_map.216.refs_2_ = bf16[2,192,1024]{2,1,0:T(8,128)(2,1)} custom-call(bf16[288,224]{1,0:T(8,128)(2,1)} %get-tuple-element.22.refs_0_, bf16[144,144]{1,0:T(8,128)(2,1)} %constant.39.clone.refs_1_, bf16[160,3072]{1,0:T(8,128)(2,1)} %get-tuple-element.25.refs_2_, bf16[24,3072]{1,0:T(8,128)(2,1)} %copy-done.4, bf16[24,3072]{1,0:T(8,128)(2,1)} %copy-done.5, ...), custom_call_target="tpu_custom_call" | custom-call | flops 7699999744 | bytes 7000000 | tf_op jit(solution)/shard_map/pallas_call | solution.py:631
  70.4 0.6 copy-done.6
  71.0 3.6 %shard_map.217 = (bf16[192,1024]{1,0:T(8,128)(2,1)}, bf16[192,1024]{1,0:T(8,128)(2,1)}) custom-call(bf16[256,1024]{1,0:T(8,128)(2,1)} %constant.44.clone.refs_0_, bf16[4,192,256]{2,1,0:T(8,128)(2,1)} %constant.45.clone.refs_1_, bf16[2,192,1024]{2,1,0:T(8,128)(2,1)} %shard_map.216.refs_2_, f32[32,8,128]{2,1,0:T(8,128)} %copy-done.6), custom_call_target="tpu_custom_call" | custom-call | flops 3300000000 | bytes 3000000 | tf_op jit(solution)/shard_map/pallas_call | solution.py:631
  (17 shorter events, 0.0 us)
Async XLA Ops:
  0.6 24.9 %copy-start.3 = (bf16[4,2,32,256]{3,2,1,0:T(8,128)(2,1)S(1)}, bf16[4,2,32,256]{3,2,1,0:T(8,128)(2,1)}, u32[]{:S(2)}) copy-start(bf16[4,2,32,256]{3,2,1,0:T(8,128)(2,1)} %constant.40.clone.refs_0_) | copy-start | bytes 393220
  5.8 19.7 %all-to-all-start = ((f32[32,8,128]{2,1,0:T(8,128)}), f32[32,8,128]{2,1,0:T(8,128)S(1)}, u32[]{:S(2)}, u32[]{:S(2)}) async-start(f32[32,8,128]{2,1,0:T(8,128)} %get-tuple-element.17), calls=%async_computation | async-start | bytes 262144 | tf_op jit(solution)/shard_map/all_to_all | solution.py:674
  16.2 24.1 %collective-permute-start = (bf16[24,3072]{1,0:T(8,128)(2,1)}, bf16[24,3072]{1,0:T(8,128)(2,1)S(1)}, u32[]{:S(2)}, u32[]{:S(2)}) collective-permute-start(bf16[24,3072]{1,0:T(8,128)(2,1)} %get-tuple-element.20), channel_id=1, source_target_pairs={{0,32},{32,0},{64,96},{96,64},{128,160},{160,128},{192,224},{224,1... | collective-permute-start | bytes 442376 | tf_op jit(solution)/shard_map/ppermute | solution.py:686
  19.5 20.2 %copy-start.7 = (f32[2,3,3]{2,0,1:T(2,128)S(1)}, f32[2,3,3]{2,0,1:T(2,128)}, u32[]{:S(2)}) copy-start(f32[2,3,3]{2,0,1:T(2,128)} %param.23) | copy-start | bytes 220
  19.5 20.8 %collective-permute-start.1 = (bf16[24,3072]{1,0:T(8,128)(2,1)}, bf16[24,3072]{1,0:T(8,128)(2,1)S(1)}, u32[]{:S(2)}, u32[]{:S(2)}) collective-permute-start(bf16[24,3072]{1,0:T(8,128)(2,1)} %get-tuple-element.21), channel_id=1, source_target_pairs={{0,480},{32,64},{64,32},{96,128},{128,96},{160,192},{192,160},{224... | collective-permute-start | bytes 442376 | tf_op jit(solution)/shard_map/ppermute | solution.py:688
  26.5 25.3 %copy-start.1 = (bf16[2,2,128,512]{3,2,1,0:T(8,128)(2,1)S(1)}, bf16[2,2,128,512]{3,2,1,0:T(8,128)(2,1)}, u32[]{:S(2)}) copy-start(bf16[2,2,128,512]{3,2,1,0:T(8,128)(2,1)} %constant.42.clone.refs_0_) | copy-start | bytes 1572868
  26.5 25.3 %copy-start.2 = (bf16[2,2,128,32]{3,2,1,0:T(8,128)(2,1)S(1)}, bf16[2,2,128,32]{3,2,1,0:T(8,128)(2,1)}, u32[]{:S(2)}) copy-start(bf16[2,2,128,32]{3,2,1,0:T(8,128)(2,1)} %constant.41.clone.refs_1_) | copy-start | bytes 98308
  26.5 25.2 %all-to-all-start.1 = ((bf16[16,32,128]{2,1,0:T(8,128)(2,1)}), bf16[16,32,128]{2,1,0:T(8,128)(2,1)S(1)}, u32[]{:S(2)}, u32[]{:S(2)}) async-start(bf16[16,32,128]{2,1,0:T(8,128)(2,1)} %shard_map.213), calls=%async_computation.1 | async-start | bytes 262144 | tf_op jit(solution)/shard_map/all_to_all | solution.py:699
  40.3 0.7 copy-start.4
  40.3 0.7 copy-start.5
  44.8 16.5 %collective-permute-start.2 = (bf16[80,3072]{1,0:T(8,128)(2,1)}, bf16[80,3072]{1,0:T(8,128)(2,1)S(1)}, u32[]{:S(2)}, u32[]{:S(2)}) collective-permute-start(bf16[80,3072]{1,0:T(8,128)(2,1)} %get-tuple-element.26), channel_id=1, source_target_pairs={{0,1},{1,2},{2,3},{3,4},{4,5},{5,6},{6,7},{7,8},{8,9},{9,10},{10,1... | collective-permute-start | bytes 1474568 | tf_op jit(solution)/shard_map/ppermute | solution.py:663
  47.5 13.8 %collective-permute-start.3 = (bf16[80,3072]{1,0:T(8,128)(2,1)}, bf16[80,3072]{1,0:T(8,128)(2,1)S(1)}, u32[]{:S(2)}, u32[]{:S(2)}) collective-permute-start(bf16[80,3072]{1,0:T(8,128)(2,1)} %get-tuple-element.27), channel_id=1, source_target_pairs={{0,31},{1,0},{2,1},{3,2},{4,3},{5,4},{6,5},{7,6},{8,7},{9,8},{10,9... | collective-permute-start | bytes 1474568 | tf_op jit(solution)/shard_map/ppermute | solution.py:663
  51.8 0.9 %copy-start = (f32[192,128]{1,0:T(8,128)S(1)}, f32[192,128]{1,0:T(8,128)}, u32[]{:S(2)}) copy-start(f32[192,128]{1,0:T(8,128)} %get-tuple-element.23.refs_2_) | copy-start | bytes 294916
  54.2 16.2 %all-to-all-start.2 = ((f32[32,8,128]{2,1,0:T(8,128)}), f32[32,8,128]{2,1,0:T(8,128)S(1)}, u32[]{:S(2)}, u32[]{:S(2)}) async-start(f32[32,8,128]{2,1,0:T(8,128)} %bitcast.3), calls=%async_computation.2 | async-start | bytes 262144 | tf_op jit(solution)/shard_map/all_to_all | solution.py:674
  61.3 0.8 %copy-start.8 = (bf16[80,3072]{1,0:T(8,128)(2,1)}, bf16[80,3072]{1,0:T(8,128)(2,1)S(1)}, u32[]{:S(2)}) copy-start(bf16[80,3072]{1,0:T(8,128)(2,1)S(1)} %collective-permute-done.2.refs_5_) | copy-start | bytes 1474564
  61.3 0.9 %copy-start.9 = (bf16[80,3072]{1,0:T(8,128)(2,1)}, bf16[80,3072]{1,0:T(8,128)(2,1)S(1)}, u32[]{:S(2)}) copy-start(bf16[80,3072]{1,0:T(8,128)(2,1)S(1)} %collective-permute-done.3.refs_6_) | copy-start | bytes 1474564
  70.4 0.7 copy-start.6
